TPU v7x, 32 devices: a whole 2x2x4 slice. The times are simulated.
32 devices in a mesh: wide: 8 (over z, y), narrow: 4 (over x, core).
Axes of the slice: x: 2, y: 2, z: 4, core: 2. Of those that a mesh axis runs over, the one named last changes fastest.
Arguments:
- boards: float32 [384, 8, 8, 256], P(('wide', 'narrow'))
- history_mask: int32 [384, 8], P(('wide', 'narrow')), may hold values 0 or 1
- kernels: float32 [2, 256, 2304], replicated, may hold values from -0.125 to 0.125
- norm_params: float32 [2, 2, 256], replicated, as said below
- norm_momenta: float32 [2, 2, 256], replicated
- left_stats: float32 [2, 256, 256], replicated
- right_stats: float32 [2, 2304, 2304], P(None, None, 'narrow')
- left_roots: float32 [2, 256, 256], replicated
- right_roots: float32 [2, 2304, 2304], P(None, None, 'narrow')
- out_cotangent: float32 [384, 8, 8, 256], P(('wide', 'narrow'))
Outputs:
- block_out: float32 [384, 8, 8, 256], P(('wide', 'narrow'))
- board_grad: float32 [384, 8, 8, 256], P(('wide', 'narrow'))
- kernel_grad: float32 [2, 256, 2304], P(None, None, 'narrow')
- new_kernels: float32 [2, 256, 2304], P(None, None, 'narrow')
- new_left: float32 [2, 256, 256], replicated
- new_right: float32 [2, 2304, 2304], P(None, None, 'narrow')
- new_momenta: float32 [2, 2, 256], replicated
- new_norm_params: float32 [2, 2, 256], replicated
Inputs may be any that keep to these rules, and one draw needn't show every extreme that they name: `norm_params`: gains positive.
All inputs are finite; a program needn't handle non-finite values. No bound on the sum of `history_mask` on one device may be relied on, other than what follows from the above.
Results may differ from a plain program's by a relative error of at most 0.012.
Values sent between devices are 32-bit elements; how exact they have to be, the bound alone decides.
A program may use at most 128 MiB of HBM per device.

v0:
```python
import jax
import jax.numpy as jnp
from jax import lax
from jax.sharding import PartitionSpec as P

HIST = 8


EPS = 1e-05
MOMENTUM = 0.9
NORM_RATE = 50.0
KERNEL_RATE = 0.1
STAT_DECAY = 0.5


def make_patches(boards_bf):
    padded = jnp.pad(boards_bf, ((0, 0), (1, 1), (1, 1), (0, 0)))
    tap_list = [
        padded[:, row_off : row_off + 8, col_off : col_off + 8, :]
        for row_off in range(3)
        for col_off in range(3)
    ]
    stacked = jnp.concatenate(tap_list, axis=3)
    return stacked.reshape(-1, stacked.shape[3])


def convolve(boards_bf, kernel_bf):
    patches = make_patches(boards_bf)
    result = lax.dot_general(
        patches, kernel_bf, (((1,), (1,)), ((), ())), preferred_element_type=jnp.float32
    )
    return (patches, result)


def flipped(kernel_bf):
    out_count = kernel_bf.shape[0]
    in_count = kernel_bf.shape[1] // 9
    grid = kernel_bf.reshape(out_count, 3, 3, in_count)[:, ::-1, ::-1, :]
    return grid.transpose(3, 1, 2, 0).reshape(in_count, 9 * out_count)


def moments(conv_rows, count):
    mean_val = lax.psum(jnp.sum(conv_rows, axis=0), ("wide", "narrow")) / count
    centred = conv_rows - mean_val
    variance = lax.psum(jnp.sum(centred * centred, axis=0), ("wide", "narrow")) / count
    return (mean_val, variance)


def forward_pass(masked, kernels_bf, norm_params, count):
    board_shape = masked.shape
    channels = board_shape[3]
    patches_one, conv_one = convolve(masked.astype(jnp.bfloat16), kernels_bf[0])
    mean_one, var_one = moments(conv_one, count)
    scale_one = lax.rsqrt(var_one + EPS)
    normed_one = (conv_one - mean_one) * scale_one
    pre_one = normed_one * norm_params[0, 0] + norm_params[0, 1]
    hidden_bf = jax.nn.gelu(pre_one).astype(jnp.bfloat16).reshape(board_shape)
    patches_two, conv_two = convolve(hidden_bf, kernels_bf[1])
    mean_two, var_two = moments(conv_two, count)
    scale_two = lax.rsqrt(var_two + EPS)
    normed_two = (conv_two - mean_two) * scale_two
    summed = masked.reshape(-1, channels) + normed_two * norm_params[1, 0] + norm_params[1, 1]
    return (patches_one, normed_one, scale_one, pre_one, patches_two, normed_two, scale_two, summed)


def norm_back(d_pre, normed, scale, gain, count):
    gain_sum, shift_sum = lax.psum(
        (jnp.sum(d_pre * normed, axis=0), jnp.sum(d_pre, axis=0)), ("wide", "narrow")
    )
    d_conv = gain * scale * (d_pre - (shift_sum + normed * gain_sum) / count)
    return (d_conv.astype(jnp.bfloat16), gain_sum, shift_sum)


def weight_terms(d_conv_bf, patches):
    return lax.dot_general(
        d_conv_bf, patches, (((0,), (0,)), ((), ())), preferred_element_type=jnp.float32
    )


def body(
    boards,
    history_mask,
    kernels,
    norm_params,
    norm_momenta,
    left_stats,
    right_stats,
    left_roots,
    right_roots,
    out_cotangent,
):
    board_shape = boards.shape
    channels = board_shape[3]
    rows = board_shape[0] * 64
    count = float(rows * lax.axis_size("wide") * lax.axis_size("narrow"))
    planes = jnp.repeat(history_mask.astype(jnp.float32), channels // HIST, axis=1)[
        :, None, None, :
    ]
    masked = boards * planes
    kernels_bf = kernels.astype(jnp.bfloat16)
    kept = forward_pass(masked, kernels_bf, norm_params, count)
    block_out = jax.nn.gelu(kept[7]).reshape(board_shape)
    kept = forward_pass(masked, kernels_bf, norm_params, count)
    patches_one, normed_one, scale_one, pre_one, patches_two, normed_two, scale_two, summed = kept
    cotangent = out_cotangent.reshape(-1, channels)
    gelu_value, gelu_pull = jax.vjp(jax.nn.gelu, summed)
    (d_sum,) = gelu_pull(cotangent)
    d_conv_two, gain_two, shift_two = norm_back(
        d_sum, normed_two, scale_two, norm_params[1, 0], count
    )
    terms_two = weight_terms(d_conv_two, patches_two)
    unused_patches, d_hidden = convolve(d_conv_two.reshape(board_shape), flipped(kernels_bf[1]))
    hidden_value, hidden_pull = jax.vjp(jax.nn.gelu, pre_one)
    (d_pre_one,) = hidden_pull(d_hidden)
    d_conv_one, gain_one, shift_one = norm_back(
        d_pre_one, normed_one, scale_one, norm_params[0, 0], count
    )
    terms_one = weight_terms(d_conv_one, patches_one)
    input_patches, d_input = convolve(d_conv_one.reshape(board_shape), flipped(kernels_bf[0]))
    board_grad = (d_sum + d_input).reshape(board_shape) * planes
    partial_value = jnp.stack([terms_one, terms_two])
    width = partial_value.shape[2] // lax.axis_size("narrow")
    start = lax.axis_index("narrow") * width
    full_sum = lax.psum(partial_value, ("wide", "narrow"))
    share = lax.dynamic_slice_in_dim(full_sum, start, width, 2)
    grad_full = full_sum / count
    kernel_grad = share / count
    norm_grad = (
        jnp.stack([jnp.stack([gain_one, shift_one]), jnp.stack([gain_two, shift_two])]) / count
    )
    new_momenta = MOMENTUM * norm_momenta + norm_grad
    new_norm_params = norm_params - NORM_RATE * new_momenta
    highest = lax.Precision.HIGHEST
    new_left = STAT_DECAY * left_stats + (1.0 - STAT_DECAY) * jnp.einsum(
        "kab,kcb->kac", grad_full, grad_full, precision=highest
    )
    new_right = STAT_DECAY * right_stats + (1.0 - STAT_DECAY) * jnp.einsum(
        "kba,kbc->kac", grad_full, kernel_grad, precision=highest
    )
    left_applied = jnp.einsum("kab,kbc->kac", left_roots, grad_full, precision=highest)
    update = jnp.einsum("kab,kbc->kac", left_applied, right_roots, precision=highest)
    kernel_share = lax.dynamic_slice_in_dim(kernels, start, width, 2)
    new_kernels = kernel_share - KERNEL_RATE * update
    return (
        block_out,
        board_grad,
        kernel_grad,
        new_kernels,
        new_left,
        new_right,
        new_momenta,
        new_norm_params,
    )


def solution(mesh):
    in_specs = (
        P(("wide", "narrow"), None, None, None),
        P(("wide", "narrow"), None),
        P(),
        P(),
        P(),
        P(),
        P(None, None, "narrow"),
        P(),
        P(None, None, "narrow"),
        P(("wide", "narrow"), None, None, None),
    )
    out_specs = (
        P(("wide", "narrow"), None, None, None),
        P(("wide", "narrow"), None, None, None),
        P(None, None, "narrow"),
        P(None, None, "narrow"),
        P(),
        P(None, None, "narrow"),
        P(),
        P(),
    )
    return jax.shard_map(body, mesh=mesh, in_specs=in_specs, out_specs=out_specs, check_vma=False)
```

profile of v0, /device:TPU:0, one launch (start us, length us, event | category | flops | bytes accessed | tf_op | source)
XLA Modules:
  0.0 496.3 jit_solution(155639338828790144)
XLA Ops:
  9.0 2.1 fusion.56
  18.9 6.0 %copy.23 = f32[2,256,2304]{1,2,0:T(8,128)} copy(f32[2,256,2304]{2,1,0:T(8,128)} %param.12) | data formatting | bytes 9437184 | tf_op args[2]
  24.9 2.6 convert_element_type.29
  27.5 1.7 fusion.57
  29.2 3.1 fusion.59
  32.3 42.0 %psum.60 = f32[256]{0:T(256)S(1)} all-reduce(f32[256]{0:T(256)S(1)} %get-tuple-element.73), channel_id=1, replica_groups=mesh['wide'=8,'narrow'=4] {'wide','narrow'}, use_global_device_ids=true, to_apply=%region_1.2 | all-reduce | flops 256 | bytes 2048 | tf_op jit(solution)/shard_map/psum | solution.py:43
  74.4 40.2 %psum.61 = f32[256]{0:T(256)S(1)} all-reduce(f32[256]{0:T(256)S(1)} %multiply_reduce_fusion.3), channel_id=1, replica_groups=mesh['wide'=8,'narrow'=4] {'wide','narrow'}, use_global_device_ids=true, to_apply=%region_3.4 | all-reduce | flops 256 | bytes 2048 | tf_op jit(solution)/shard_map/psum | solution.py:45
  115.9 1.5 copy.24
  122.0 39.9 %psum.64 = f32[256]{0:T(256)S(1)} all-reduce(f32[256]{0:T(256)S(1)} %get-tuple-element.75), channel_id=1, replica_groups=mesh['wide'=8,'narrow'=4] {'wide','narrow'}, use_global_device_ids=true, to_apply=%region_5.6 | all-reduce | flops 256 | bytes 2048 | tf_op jit(solution)/shard_map/psum | solution.py:43
  162.1 40.1 %psum.78 = f32[256]{0:T(256)S(1)} all-reduce(f32[256]{0:T(256)S(1)} %multiply_reduce_fusion.2), channel_id=1, replica_groups=mesh['wide'=8,'narrow'=4] {'wide','narrow'}, use_global_device_ids=true, to_apply=%region_7.8 | all-reduce | flops 256 | bytes 2048 | tf_op jit(solution)/shard_map/psum | solution.py:45
  202.1 3.0 fusion.52
  205.2 40.1 %all-reduce.5 = (f32[256]{0:T(256)S(1)}, f32[256]{0:T(256)S(1)}) all-reduce(f32[256]{0:T(256)S(1)} %get-tuple-element.27, f32[256]{0:T(256)S(1)} %get-tuple-element.26), channel_id=1, replica_groups=mesh['wide'=8,'narrow'=4] {'wide','narrow'}, use_global_device_ids=true, to_apply=%region_11.12 | all-reduce | flops 512 | bytes 4096 | tf_op jit(solution)/shard_map/psum | solution.py:67
  245.4 4.6 convolution_bitcast_fusion
  251.9 1.6 fusion.51
  253.5 40.1 %all-reduce.4 = (f32[256]{0:T(256)S(1)}, f32[256]{0:T(256)S(1)}) all-reduce(f32[256]{0:T(256)S(1)} %get-tuple-element.25, f32[256]{0:T(256)S(1)} %get-tuple-element.24), channel_id=1, replica_groups=mesh['wide'=8,'narrow'=4] {'wide','narrow'}, use_global_device_ids=true, to_apply=%region_15.16 | all-reduce | flops 512 | bytes 4096 | tf_op jit(solution)/shard_map/psum | solution.py:67
  293.8 3.3 convolution_bitcast_fusion.1
  297.1 2.5 pad_maximum_fusion
  300.9 1.5 copy.25
  306.7 138.4 %all-reduce.8.cloned.1.call-done = f32[2,256,2304]{2,1,0:T(8,128)} async-done(((f32[2,256,2304]{2,1,0:T(8,128)}), f32[2,256,2304]{2,1,0:T(8,128)}) %all-reduce.8.cloned.1.call-update) | async-done | bytes 4718608 | tf_op jit(solution)/shard_map/psum | solution.py:124
  445.1 1.8 dynamic-slice_multiply_fusion
  448.3 10.1 %fusion.3 = f32[2,2304,256]{2,1,0:T(8,128)S(1)} fusion(f32[2,256,256]{2,1,0:T(8,128)S(1)} %copy-done, f32[2,256,2304]{2,1,0:T(8,128)} %all-reduce.8.cloned.1.call-done), kind=kOutput, calls=%fused_computation.5 | convolution fusion | flops 3625058304 | bytes 9961472 | tf_op jit(solution)/shard_map/kab,kbc->kac/dot_general | solution.py:140
  458.4 12.6 %fusion.8 = f32[2,256,576]{1,2,0:T(8,128)} fusion(f32[2,2304,256]{2,1,0:T(8,128)S(1)} %fusion.3, f32[2,2304,576]{1,2,0:T(8,128)} %param.18, f32[2,256,2304]{1,2,0:T(8,128)} %copy.23, s32[]{:T(128)S(6)} %select_n.4), kind=kOutput, calls=%fused_computation.45 | convolution fusion | flops 8154316800 | bytes 17694724 | tf_op jit(solution)/shard_map/kab,kbc->kac/dot_general | solution.py:141
  471.0 5.6 %fusion.12 = f32[2,256,256]{2,1,0:T(8,128)} fusion(f32[2,256,256]{2,1,0:T(8,128)S(1)} %copy-done.9, f32[2,256,2304]{2,1,0:T(8,128)S(1)} %bitcast.102), kind=kOutput, calls=%fused_computation.49 | convolution fusion | flops 3625320448 | bytes 5767168 | tf_op jit(solution)/shard_map/kab,kcb->kac/dot_general | solution.py:134
  476.7 12.3 %add_multiply_fusion = f32[2,2304,576]{1,2,0:T(8,128)} fusion(f32[2,2304,576]{1,2,0:T(8,128)S(1)} %bitcast.104, f32[2,256,576]{2,1,0:T(8,128)S(1)} %dynamic-slice_multiply_fusion, f32[2,256,2304]{2,1,0:T(8,128)S(1)} %bitcast.102), kind=kOutput, calls=%fused_computation | convolution fusion | flops 8160215040 | bytes 27131904 | tf_op jit(solution)/shard_map/kba,kbc->kac/dot_general | solution.py:137
  (99 shorter events, 24.7 us)
Async XLA Ops:
  7.2 441.1 %copy-start = (f32[2,256,256]{2,1,0:T(8,128)S(1)}, f32[2,256,256]{2,1,0:T(8,128)}, u32[]{:S(2)}) copy-start(f32[2,256,256]{2,1,0:T(8,128)} %param.17) | copy-start | bytes 1572868
  7.2 437.9 %all-reduce.8.cloned.1.call-start = ((), (), s32[]{:S(2)}) async-start(), calls=%async_computation | async-start | bytes 9437184 | tf_op jit(solution)/shard_map/psum | solution.py:124
  27.5 4.8 copy-start.1
  118.5 1.7 copy-start.2
  120.2 1.8 copy-start.4
  205.1 44.9 %copy-start.5 = (f32[768,256]{1,0:T(8,128)}, f32[768,256]{1,0:T(8,128)S(1)}, u32[]{:S(2)}) copy-start(f32[768,256]{1,0:T(8,128)S(1)} %get-tuple-element.35) | copy-start | bytes 2359300
  250.6 1.3 copy-start.7
  293.8 3.3 copy-start.3
  303.1 0.7 copy-start.10
  303.1 0.7 copy-start.11
  303.1 1.3 copy-start.6
  303.1 1.5 copy-start.8
  448.3 22.8 %slice-start = ((s8[4718592]{0:T(1024)(128)(4,1)}), s8[4194304]{0:T(1024)(128)(4,1)S(1)}, s32[]{:S(2)}) async-start(s8[4718592]{0:T(1024)(128)(4,1)} %bitcast.101), calls=%async_computation.1 | async-start | bytes 8388608
  448.3 28.4 %slice-start.2 = ((s8[10616832]{0:T(1024)(128)(4,1)}), s8[4194304]{0:T(1024)(128)(4,1)S(1)}, s32[]{:S(2)}) async-start(s8[10616832]{0:T(1024)(128)(4,1)} %bitcast.103), calls=%async_computation.3 | async-start | bytes 8388608
  458.4 12.7 %slice-start.1 = ((s8[4718592]{0:T(1024)(128)(4,1)}), s8[524288]{0:T(1024)(128)(4,1)S(1)}, s32[]{:S(2)}) async-start(s8[4718592]{0:T(1024)(128)(4,1)} %bitcast.101), calls=%async_computation.2 | async-start | bytes 1048576
  458.4 12.7 %copy-start.9 = (f32[2,256,256]{2,1,0:T(8,128)S(1)}, f32[2,256,256]{2,1,0:T(8,128)}, u32[]{:S(2)}) copy-start(f32[2,256,256]{2,1,0:T(8,128)} %param.15) | copy-start | bytes 1572868
  458.4 18.3 %slice-start.3 = ((s8[10616832]{0:T(1024)(128)(4,1)}), s8[4194304]{0:T(1024)(128)(4,1)S(1)}, s32[]{:S(2)}) async-start(s8[10616832]{0:T(1024)(128)(4,1)} %bitcast.103), calls=%async_computation.4 | async-start | bytes 8388608
  458.4 18.3 %slice-start.4 = ((s8[10616832]{0:T(1024)(128)(4,1)}), s8[2228224]{0:T(1024)(128)(4,1)S(1)}, s32[]{:S(2)}) async-start(s8[10616832]{0:T(1024)(128)(4,1)} %bitcast.103), calls=%async_computation.5 | async-start | bytes 4456448
Sparse Core Ops, SparseCore 0:
  299.7 145.2 all-reduce.7
where the time goes:
time: 504 us; the launch traced here: 496 us
  blocking collectives  242 us (48%)
  waiting for transfers between devices  138 us (27%)
  matrix products  55.3 us (11%)
  local copies, waits for them, and re-layouts  29.5 us (6%)
  other arithmetic  15.7 us (3%)
  between operations  14.9 us (3%)
    psum x1, waiting for transfers between devices, body(): full_sum = lax.psum(partial_value, ('wide', 'narrow'))  138 us
    psum x2, blocking collectives, moments(): mean_val = lax.psum(jnp.sum(conv_rows, axis=0), ('wide', 'narrow')) / count  81.9 us
    psum x2, blocking collectives, moments(): lax.psum(jnp.sum(centred * centred, axis=0), ('wide', 'narrow')) / count  80.2 us
    psum x2, blocking collectives, norm_back(): lax.psum((jnp.sum(d_pre * normed, axis=0), jnp.sum(d_pre, axis=0)), ('wid...  80.2 us
    unnamed x67, local copies, waits for them, and re-layouts  18.3 us
    dot_general x1, matrix products, body(): jnp.einsum('kab,kbc->kac', left_applied, right_roots, precision=highest)  12.6 us
    dot_general x1, matrix products, body(): jnp.einsum('kba,kbc->kac', grad_full, kernel_grad, precision=highest)  12.3 us
  transfers between devices with their start and end apart: 1, of which 1 were waited for; matrix products, arithmetic and copies ran while one was open for 1% of the time, Pallas kernels for 0%

commit v1 on v0

v1 whole, which is shorter than its diff:
```python
import functools
import math

import jax
import jax.numpy as jnp
from jax import lax
from jax.experimental import pallas as pl
from jax.experimental.pallas import tpu as pltpu
from jax.sharding import PartitionSpec as P

EPS = 1e-05
MOMENTUM = 0.9
NORM_RATE = 50.0
KERNEL_RATE = 0.1
STAT_DECAY = 0.5

SIDE = 8
CUBE = 0.044715
ROOT = math.sqrt(2.0 / math.pi)
MESH = pl.DeviceIdType.MESH
F32 = jnp.float32
BF16 = jnp.bfloat16
MIB = 2**20


def dot(lhs, rhs, lhs_dim, rhs_dim):
    return lax.dot_general(
        lhs, rhs, (((lhs_dim,), (rhs_dim,)), ((), ())), preferred_element_type=F32
    )


def gelu_tanh(v):
    return jnp.tanh(ROOT * (v + CUBE * (v * v * v)))


def gelu_slope(v, t):
    inner = ROOT * (1.0 + (3.0 * CUBE) * (v * v))
    return 0.5 * (1.0 + t) + (0.5 * v) * ((1.0 - t * t) * inner)


def flip(index, bit):
    return index + (1 - 2 * ((index // (1 << bit)) % 2)) * (1 << bit)


def bit_of(index, bit):
    return (index // (1 << bit)) % 2


def pick(taken, one, other):
    return taken * one + (1 - taken) * other


def fused_kernel(
    dims,
    boards,
    mask_t,
    kernels,
    params,
    momenta,
    left_stats,
    left_roots,
    right_stats,
    right_roots,
    cotangent,
    g_full,
    stats_v,
    roots_v,
    lstats_v,
    lroots_v,
    kt,
    bo,
    bg,
    new_momenta,
    new_params,
    bd,
    ct,
    mk,
    par,
    mom,
    kf,
    wb,
    ktmp,
    x_one,
    x_two,
    dgrid,
    h_one,
    slope_one,
    h_two,
    d_sum,
    d_hid,
    gp,
    red,
    half_in,
    first_in,
    second_in,
    depth_in,
    more_in,
    load_sem,
    red_send,
    red_recv,
    g_send,
    g_recv,
):
    nw, nn, pos, chan = dims
    line = pos * SIDE
    rows = line * SIDE
    count = float(rows * nw * nn)
    taps = 9 * chan
    chunk = 3 * chan
    part0, part1, part2, part3 = chunk // 2, chunk // 4, chunk // 8, chunk // 32
    wide, narrow = lax.axis_index("wide"), lax.axis_index("narrow")
    me = wide * nn + narrow
    extra_bits = list(range(3, nw.bit_length() - 1))

    def load(slot, src, dst):
        copy = pltpu.make_async_copy(src, dst, load_sem.at[slot])
        copy.start()
        return copy

    got_k0 = load(0, kernels.at[0], kf.at[0])
    got_mask = load(1, mask_t, mk)
    got_boards = [load(2 + i, boards.at[:, i], bd.at[i]) for i in range(SIDE)]
    got_par = load(10, params, par)

    def each_other(act):
        if nw * nn <= 32:
            for k in range(nw * nn - 1, 0, -1):
                w, n = wide, narrow
                for b in range(nw.bit_length() - 1):
                    if (k // nn) >> b & 1:
                        w = flip(w, b) if b == 0 else w + (flip(wide, b) - wide)
                for b in range(nn.bit_length() - 1):
                    if (k % nn) >> b & 1:
                        n = n + (flip(narrow, b) - narrow)
                act((w, n))
        else:

            @pl.loop(1, nw * nn)
            def _(k):
                other = lax.rem(me + k, nw * nn)
                act((other // nn, lax.rem(other, nn)))

    barrier = pltpu.get_barrier_semaphore()
    each_other(
        lambda dev: pl.semaphore_signal(barrier, inc=1, device_id=dev, device_id_type=MESH)
    )

    def share(slot, value):
        red[slot, me] = value

        def send(dev):
            pltpu.make_async_remote_copy(
                src_ref=red.at[slot, me],
                dst_ref=red.at[slot, me],
                send_sem=red_send.at[slot],
                recv_sem=red_recv.at[slot],
                device_id=dev,
                device_id_type=MESH,
            ).start()

        each_other(send)

    def collect(slot):
        others = red.at[slot, pl.ds(0, nw * nn - 1)]
        pltpu.make_async_copy(others, others, red_recv.at[slot]).wait()
        pltpu.make_async_copy(others, others, red_send.at[slot]).wait()
        return red[slot]

    def moments(slot):
        got = collect(slot)
        means, spreads = got[:, 0, :], got[:, 1, :]
        mean = jnp.sum(means, axis=0, keepdims=True) * (1.0 / (nw * nn))
        gap = means - mean
        spread = jnp.sum(spreads, axis=0, keepdims=True) + float(rows) * jnp.sum(
            gap * gap, axis=0, keepdims=True
        )
        return mean, lax.rsqrt(spread / count + EPS)

    def totals(slot):
        got = collect(slot)
        return (
            jnp.sum(got[:, 0, :], axis=0, keepdims=True),
            jnp.sum(got[:, 1, :], axis=0, keepdims=True),
        )

    def local_moments(ref):
        total = jnp.sum(ref[...], axis=0, keepdims=True)
        mean = total * (1.0 / rows)
        gap = ref[...] - mean
        return jnp.concatenate([mean, jnp.sum(gap * gap, axis=0, keepdims=True)], axis=0)

    column = lax.broadcasted_iota(jnp.int32, (pos, SIDE, chan), 1)

    def put_shifted(grid, i, value):
        cube = value.reshape(pos, SIDE, chan)
        before = jnp.where(column == 0, 0.0, pltpu.roll(cube, 1, 1))
        after = jnp.where(column == SIDE - 1, 0.0, pltpu.roll(cube, SIDE - 1, 1))
        at = pl.ds(pl.multiple_of((i + 1) * line, 16), line)
        grid[at, 0:chan] = before.reshape(line, chan).astype(BF16)
        grid[at, chan : 2 * chan] = value.astype(BF16)
        grid[at, 2 * chan : 3 * chan] = after.reshape(line, chan).astype(BF16)

    def at_line(i):
        return pl.ds(pl.multiple_of(i * line, 8), line)

    def conv(grid, k):
        return sum(
            dot(
                grid[a * line : a * line + rows, :],
                wb[k, :, a * chunk : (a + 1) * chunk],
                1,
                1,
            )
            for a in range(3)
        )

    def conv_back(grid, k):
        result = None
        for a in range(3):
            for b in range(3):
                tap = 3 * (2 - a) + (2 - b)
                term = dot(
                    grid[a * line : a * line + rows, b * chan : (b + 1) * chan],
                    wb[k, :, tap * chan : (tap + 1) * chan],
                    1,
                    0,
                )
                result = term if result is None else result + term
        return result

    core = bit_of(narrow, 0)
    x_bit, y_bit = bit_of(narrow, 1), bit_of(wide, 0)
    z_low, z_high = bit_of(wide, 1), bit_of(wide, 2)
    z_pos = z_low + 2 * z_high
    core_dev = (wide, flip(narrow, 0))
    x_dev = (wide, flip(narrow, 1))
    y_dev = (flip(wide, 0), narrow)
    first_dev = (pick(core, y_dev[0], x_dev[0]), pick(core, y_dev[1], x_dev[1]))
    second_dev = (pick(core, x_dev[0], y_dev[0]), pick(core, x_dev[1], y_dev[1]))
    first_bit, second_bit = pick(core, y_bit, x_bit), pick(core, x_bit, y_bit)

    def z_other(q):
        low = 1 - z_low if q & 1 else z_low
        high = 1 - z_high if q & 2 else z_high
        return low + 2 * high

    sends = []

    def remote(k, a, slot, src, dst, dev):
        copy = pltpu.make_async_remote_copy(
            src_ref=src,
            dst_ref=dst,
            send_sem=g_send.at[k, a, slot],
            recv_sem=g_recv.at[k, a, slot],
            device_id=dev,
            device_id_type=MESH,
        )
        copy.start()
        sends.append(copy)
        return copy

    def exchange(k, a):
        base = a * chunk
        off0 = base + core * part0
        off1 = off0 + first_bit * part1
        off2 = off1 + second_bit * part2
        off3 = off2 + z_pos * part3
        live = {}

        def at(start, size):
            return pl.ds(pl.multiple_of(start, 8), size)

        def begin():
            src = gp.at[k, at(base + (1 - core) * part0, part0)]
            live["c"] = remote(k, a, 0, src, half_in.at[k, a], core_dev)

        def after_core():
            live["c"].wait_recv()
            own = at(off0, part0)
            gp[k, own] = gp[k, own] + half_in[k, a]
            src = gp.at[k, at(off0 + (1 - first_bit) * part1, part1)]
            live["1"] = remote(k, a, 1, src, first_in.at[k, a], first_dev)

        def after_first():
            live["1"].wait_recv()
            own = at(off1, part1)
            gp[k, own] = gp[k, own] + first_in[k, a]
            src = gp.at[k, at(off1 + (1 - second_bit) * part2, part2)]
            live["2"] = remote(k, a, 2, src, second_in.at[k, a], second_dev)

        def after_second():
            live["2"].wait_recv()
            own = at(off2, part2)
            gp[k, own] = gp[k, own] + second_in[k, a]
            live["z"] = []
            for q in (3, 2, 1):
                other = z_other(q)
                dev = (wide + 2 * (other - z_pos), narrow)
                src = gp.at[k, at(off2 + other * part3, part3)]
                live["z"].append(remote(k, a, 2 + q, src, depth_in.at[k, a, q - 1], dev))

        def after_depth():
            for copy in live["z"]:
                copy.wait_recv()
            own = at(off3, part3)
            value = ((gp[k, own] + depth_in[k, a, 0]) + depth_in[k, a, 1]) + depth_in[k, a, 2]
            for e, b in enumerate(extra_bits):
                gp[k, own] = value
                copy = remote(
                    k, a, 12 + e, gp.at[k, own], more_in.at[k, a, e], (flip(wide, b), narrow)
                )
                copy.wait_recv()
                copy.wait_send()
                sends.pop()
                value = value + more_in[k, a, e]
            g_full[k, own] = value * (1.0 / count)
            live["gz"] = []
            for q in (3, 2, 1):
                dev = (wide + 2 * (z_other(q) - z_pos), narrow)
                live["gz"].append(
                    remote(k, a, 5 + q, g_full.at[k, own], g_full.at[k, own], dev)
                )

        def back_depth():
            for copy in live["gz"]:
                copy.wait_recv()
            ref = g_full.at[k, at(off2, part2)]
            live["g2"] = remote(k, a, 9, ref, ref, second_dev)

        def back_second():
            live["g2"].wait_recv()
            ref = g_full.at[k, at(off1, part1)]
            live["g1"] = remote(k, a, 10, ref, ref, first_dev)

        def back_first():
            live["g1"].wait_recv()
            ref = g_full.at[k, at(off0, part0)]
            live["gc"] = remote(k, a, 11, ref, ref, core_dev)

        def end():
            live["gc"].wait_recv()

        return [
            begin,
            after_core,
            after_first,
            after_second,
            after_depth,
            back_depth,
            back_second,
            back_first,
            end,
        ]

    events = {(k, a): exchange(k, a) for k in range(2) for a in range(3)}

    def do(k, step):
        for a in range(3):
            events[k, a][step]()

    empty = jnp.zeros((line, 3 * chan), BF16)
    for grid in (x_one, x_two, dgrid):
        grid[0:line, :] = empty
        grid[line + rows : 2 * line + rows, :] = empty

    got_mask.wait()
    hist = mk.shape[0]
    width = chan // hist
    spot = lax.broadcasted_iota(jnp.int32, (pos, line), 1)
    owner = SIDE * lax.broadcasted_iota(jnp.int32, (pos, line), 0)
    spread_pos = jnp.where((spot >= owner) & (spot < owner + SIDE), 1.0, 0.0).astype(BF16)
    spot = lax.broadcasted_iota(jnp.int32, (hist, chan), 1)
    owner = width * lax.broadcasted_iota(jnp.int32, (hist, chan), 0)
    spread_chan = jnp.where((spot >= owner) & (spot < owner + width), 1.0, 0.0).astype(BF16)
    by_row = dot(mk[...].astype(F32).astype(BF16), spread_pos, 1, 0).astype(BF16)
    planes = dot(by_row, spread_chan, 0, 0)

    got_k0.wait()
    wb[0] = kf[0].astype(BF16)
    got_k1 = load(11, kernels.at[1], kf.at[1])
    got_ct = [load(12 + i, cotangent.at[:, i], ct.at[i]) for i in range(SIDE)]
    for i in range(SIDE):
        got_boards[i].wait()
        value = bd[i].reshape(line, chan) * planes
        bd[i] = value.reshape(pos, SIDE, chan)
        put_shifted(x_one, i, value)

    h_one[...] = conv(x_one, 0)
    local = local_moments(h_one)
    pl.semaphore_wait(barrier, nw * nn - 1)
    share(0, local)

    got_par.wait()
    late = [
        load(20, momenta, mom),
        load(21, left_stats, lstats_v),
        load(22, left_roots, lroots_v),
        load(23, right_roots, roots_v),
        load(24, right_stats, stats_v),
    ]
    got_k1.wait()
    wb[1] = kf[1].astype(BF16)

    def keep_share(k):
        share_width = kt.shape[1]
        span = ktmp.shape[0]
        start = narrow * share_width
        block = (start // 128) * 128
        ktmp[...] = kf[k, :, pl.ds(pl.multiple_of(block, 128), span)].T
        kt[k] = ktmp[pl.ds(pl.multiple_of(start - block, 8), share_width), :]

    keep_share(0)
    keep_share(1)

    gain_one, shift_one = par[0, 0:1, :], par[0, 1:2, :]
    gain_two, shift_two = par[1, 0:1, :], par[1, 1:2, :]

    mean_one, inv_one = moments(0)

    @pl.loop(0, SIDE)
    def _(i):
        at = at_line(i)
        normed = (h_one[at, :] - mean_one) * inv_one
        h_one[at, :] = normed
        pre = normed * gain_one + shift_one
        put_shifted(x_two, i, (0.5 * pre) * (1.0 + gelu_tanh(pre)))

    h_two[...] = conv(x_two, 1)
    share(1, local_moments(h_two))

    @pl.loop(0, SIDE)
    def _(i):
        at = at_line(i)
        pre = h_one[at, :] * gain_one + shift_one
        slope_one[at, :] = gelu_slope(pre, gelu_tanh(pre))

    for copy in got_ct:
        copy.wait()
    mean_two, inv_two = moments(1)

    def fold(value):
        return jnp.sum(value.reshape(pos, SIDE, chan), axis=0)

    nothing = jnp.zeros((SIDE, chan), F32)

    def close(gain_sum, shift_sum):
        return jnp.concatenate(
            [
                jnp.sum(gain_sum, axis=0, keepdims=True),
                jnp.sum(shift_sum, axis=0, keepdims=True),
            ],
            axis=0,
        )

    def out_line(i, carry):
        at = at_line(i)
        normed = (h_two[at, :] - mean_two) * inv_two
        h_two[at, :] = normed
        summed = bd[i].reshape(line, chan) + normed * gain_two + shift_two
        t = gelu_tanh(summed)
        bo[i] = ((0.5 * summed) * (1.0 + t)).reshape(pos, SIDE, chan)
        slope = ct[i].reshape(line, chan) * gelu_slope(summed, t)
        d_sum[at, :] = slope
        return carry[0] + fold(slope * normed), carry[1] + fold(slope)

    share(2, close(*lax.fori_loop(0, SIDE, out_line, (nothing, nothing))))

    gain_two_sum, shift_two_sum = totals(2)
    scale_two = gain_two * inv_two

    @pl.loop(0, SIDE)
    def _(i):
        at = at_line(i)
        lost = (shift_two_sum + h_two[at, :] * gain_two_sum) * (1.0 / count)
        put_shifted(dgrid, i, scale_two * (d_sum[at, :] - lost))

    def weight_chunk(grid, k, a):
        gp[k, a * chunk : (a + 1) * chunk, :] = dot(
            grid[a * line : a * line + rows, :], dgrid[line : line + rows, chan : 2 * chan], 0, 0
        )
        events[k, a][0]()

    for a in range(3):
        weight_chunk(x_two, 1, a)
    d_hid[...] = conv_back(dgrid, 1)
    do(1, 1)

    def pre_line(i, carry):
        at = at_line(i)
        d_pre = d_hid[at, :] * slope_one[at, :]
        d_hid[at, :] = d_pre
        return carry[0] + fold(d_pre * h_one[at, :]), carry[1] + fold(d_pre)

    share(3, close(*lax.fori_loop(0, SIDE, pre_line, (nothing, nothing))))
    gain_one_sum, shift_one_sum = totals(3)
    scale_one = gain_one * inv_one

    @pl.loop(0, SIDE)
    def _(i):
        at = at_line(i)
        lost = (shift_one_sum + h_one[at, :] * gain_one_sum) * (1.0 / count)
        put_shifted(dgrid, i, scale_one * (d_hid[at, :] - lost))

    for a in range(3):
        weight_chunk(x_one, 0, a)
    do(1, 2)
    d_hid[...] = conv_back(dgrid, 0)
    do(0, 1)
    for i in range(SIDE):
        at = at_line(i)
        bg[i] = ((d_sum[at, :] + d_hid[at, :]) * planes).reshape(pos, SIDE, chan)

    for copy in late:
        copy.wait()
    norm_grad = [
        jnp.concatenate([gain_one_sum, shift_one_sum], axis=0),
        jnp.concatenate([gain_two_sum, shift_two_sum], axis=0),
    ]
    for k in range(2):
        value = MOMENTUM * mom[k] + norm_grad[k] * (1.0 / count)
        new_momenta[k] = value
        new_params[k] = par[k] - NORM_RATE * value

    do(1, 3)
    do(0, 2)
    do(1, 4)
    do(0, 3)
    do(1, 5)
    do(0, 4)
    do(1, 6)
    do(0, 5)
    do(1, 7)
    do(0, 6)
    do(1, 8)
    do(0, 7)
    do(0, 8)
    for copy in sends:
        copy.wait_send()


def finish_kernel(
    dims,
    g_full,
    stats,
    roots,
    lstats,
    lroots,
    kt,
    bo,
    bg,
    momenta,
    params,
    o_block,
    o_board,
    o_grad,
    o_kernel,
    o_left,
    o_right,
    o_momenta,
    o_params,
    gb,
    nr,
    nk,
    nl,
    sem,
):
    chan = dims[3]
    chunk = 3 * chan
    share_width = kt.shape[1]
    start = pl.multiple_of(lax.axis_index("narrow") * share_width, 8)
    copies = []

    def put(src, dst):
        copy = pltpu.make_async_copy(src, dst, sem.at[len(copies)])
        copy.start()
        copies.append(copy)

    for k in range(2):
        put(g_full.at[k, pl.ds(start, share_width)], o_grad.at[k])
        gb[k] = g_full[k].astype(BF16)
        own = g_full[k, pl.ds(start, share_width), :].astype(BF16)
        for q in range(3):
            cols = pl.ds(q * chunk, chunk)
            term = dot(own, gb[k, cols, :], 1, 1)
            nr[k, q] = STAT_DECAY * stats[k, :, cols] + (1.0 - STAT_DECAY) * term
            put(nr.at[k, q], o_right.at[k, :, cols])
        if k == 0:
            for i in range(SIDE):
                put(bo.at[i], o_block.at[:, i])
                put(bg.at[i], o_board.at[:, i])
            put(momenta, o_momenta)
            put(params, o_params)
    for k in range(2):
        term = dot(gb[k], gb[k], 0, 0)
        nl[k] = STAT_DECAY * lstats[k] + (1.0 - STAT_DECAY) * term
        put(nl.at[k], o_left.at[k])
        mixed = dot(roots[k].astype(BF16), gb[k], 1, 0)
        update = dot(mixed.astype(BF16), lroots[k].astype(BF16), 1, 1)
        nk[k] = kt[k] - KERNEL_RATE * update
        put(nk.at[k], o_kernel.at[k])
    for copy in copies:
        copy.wait()


def body(
    nw,
    nn,
    boards,
    history_mask,
    kernels,
    norm_params,
    norm_momenta,
    left_stats,
    right_stats,
    left_roots,
    right_roots,
    out_cotangent,
):
    pos, chan = boards.shape[0], boards.shape[3]
    kin = kernels.shape[2]
    share_width = right_stats.shape[2]
    line = pos * SIDE
    rows = line * SIDE
    chunk = 3 * chan
    ndev = nw * nn
    extra = max(nw.bit_length() - 4, 0)
    dims = (nw, nn, pos, chan)
    hbm = pl.BlockSpec(memory_space=pl.ANY)
    vmem = pl.BlockSpec(memory_space=pltpu.VMEM)
    span = -(-(share_width + 64) // 128) * 128
    board_shape = (SIDE, pos, SIDE, chan)

    kept = [
        (2, kin, chan),
        (2, share_width, kin),
        (2, share_width, kin),
        (2, chan, chan),
        (2, chan, chan),
        (2, share_width, chan),
        board_shape,
        board_shape,
        (2, 2, chan),
        (2, 2, chan),
    ]
    fused = pl.pallas_call(
        functools.partial(fused_kernel, dims),
        out_shape=[pltpu.VMEM(shape, F32) for shape in kept],
        in_specs=[hbm] * 10,
        out_specs=[vmem] * len(kept),
        scratch_shapes=[
            pltpu.VMEM(board_shape, F32),
            pltpu.VMEM(board_shape, F32),
            pltpu.VMEM(history_mask.shape[::-1], jnp.int32),
            pltpu.VMEM((2, 2, chan), F32),
            pltpu.VMEM((2, 2, chan), F32),
            pltpu.VMEM((2, chan, kin), F32),
            pltpu.VMEM((2, chan, kin), BF16),
            pltpu.VMEM((span, chan), F32),
            pltpu.VMEM((rows + 2 * line, chunk), BF16),
            pltpu.VMEM((rows + 2 * line, chunk), BF16),
            pltpu.VMEM((rows + 2 * line, chunk), BF16),
            pltpu.VMEM((rows, chan), F32),
            pltpu.VMEM((rows, chan), F32),
            pltpu.VMEM((rows, chan), F32),
            pltpu.VMEM((rows, chan), F32),
            pltpu.VMEM((rows, chan), F32),
            pltpu.VMEM((2, kin, chan), F32),
            pltpu.VMEM((4, ndev, 2, chan), F32),
            pltpu.VMEM((2, 3, chunk // 2, chan), F32),
            pltpu.VMEM((2, 3, chunk // 4, chan), F32),
            pltpu.VMEM((2, 3, chunk // 8, chan), F32),
            pltpu.VMEM((2, 3, 3, chunk // 32, chan), F32),
            pltpu.VMEM((2, 3, max(extra, 1), chunk // 32, chan), F32),
            pltpu.SemaphoreType.DMA((25,)),
            pltpu.SemaphoreType.DMA((4,)),
            pltpu.SemaphoreType.DMA((4,)),
            pltpu.SemaphoreType.DMA((2, 3, 12 + extra)),
            pltpu.SemaphoreType.DMA((2, 3, 12 + extra)),
        ],
        compiler_params=pltpu.CompilerParams(
            collective_id=0, has_side_effects=True, vmem_limit_bytes=34 * MIB
        ),
        name="fused_passes",
    )
    held = fused(
        boards,
        history_mask.T,
        kernels,
        norm_params,
        norm_momenta,
        left_stats,
        left_roots,
        jnp.swapaxes(right_stats, 1, 2),
        jnp.swapaxes(right_roots, 1, 2),
        out_cotangent,
    )
    finish = pl.pallas_call(
        functools.partial(finish_kernel, dims),
        out_shape=[
            pltpu.HBM(boards.shape, F32),
            pltpu.HBM(boards.shape, F32),
            pltpu.HBM((2, share_width, chan), F32),
            pltpu.HBM((2, share_width, chan), F32),
            pltpu.HBM((2, chan, chan), F32),
            pltpu.HBM((2, share_width, kin), F32),
            pltpu.HBM((2, 2, chan), F32),
            pltpu.HBM((2, 2, chan), F32),
        ],
        in_specs=[vmem] * len(kept),
        out_specs=[hbm] * 8,
        scratch_shapes=[
            pltpu.VMEM((2, kin, chan), BF16),
            pltpu.VMEM((2, 3, share_width, chunk), F32),
            pltpu.VMEM((2, share_width, chan), F32),
            pltpu.VMEM((2, chan, chan), F32),
            pltpu.SemaphoreType.DMA((32,)),
        ],
        compiler_params=pltpu.CompilerParams(vmem_limit_bytes=24 * MIB),
        name="finish",
    )
    block_out, board_grad, grad, kernel, left, right, momenta, params = finish(*held)
    return (
        block_out,
        board_grad,
        jnp.swapaxes(grad, 1, 2),
        jnp.swapaxes(kernel, 1, 2),
        left,
        jnp.swapaxes(right, 1, 2),
        momenta,
        params,
    )


def solution(mesh):
    nw, nn = mesh.shape["wide"], mesh.shape["narrow"]
    boards = P(("wide", "narrow"), None, None, None)
    columns = P(None, None, "narrow")
    in_specs = (
        boards,
        P(("wide", "narrow"), None),
        P(),
        P(),
        P(),
        P(),
        columns,
        P(),
        columns,
        boards,
    )
    out_specs = (boards, boards, columns, columns, P(), columns, P(), P())
    return jax.shard_map(
        functools.partial(body, nw, nn),
        mesh=mesh,
        in_specs=in_specs,
        out_specs=out_specs,
        check_vma=False,
    )
```

time: 504 us -> 121 us (0.24); the launches traced: 496 us -> 121 us
  blocking collectives: 242 us -> 0 us
  waiting for transfers between devices: 138 us -> 0 us
  Pallas kernels: 0 us -> 99.5 us
  matrix products: 55.3 us -> 0 us
  other arithmetic: 15.7 us -> 0 us
  between operations: 14.9 us -> 0.82 us
  local copies, waits for them, and re-layouts: 29.5 us -> 20.7 us
    psum x6 -> x0, blocking collectives: 242 us -> none  [the longest x2 81.9 us: moments(): mean_val = lax.psum(jnp.sum(conv_rows, axis=0), ('wide', 'narrow')) / count]
    psum x1 -> x0, waiting for transfers between devices: 138 us -> none  [body(): full_sum = lax.psum(partial_value, ('wide', 'narrow'))]
    pallas_call x0 -> x2, Pallas kernels: none -> 99.5 us  [the longest x1 92.5 us: body(): fused(boards, history_mask.T, kernels, norm_params, norm_momenta, left_st...]
    dot_general x10 -> x0, matrix products: 55.3 us -> none  [the longest x1 12.6 us: body(): jnp.einsum('kab,kbc->kac', left_applied, right_roots, precision=highest)]
    convert_element_type x6 -> x0, other arithmetic: 6.2 us -> none  [the longest x1 2.57 us: body(): kernels_bf = kernels.astype(jnp.bfloat16)]
    transpose x4 -> x0, local copies, waits for them, and re-layouts: 5.77 us -> none  [flipped(): return grid.transpose(3, 1, 2, 0).reshape(in_count, 9 * out_count)]
    unnamed x67 -> x12, local copies, waits for them, and re-layouts: 18.3 us -> 20.7 us
  transfers between devices with their start and end apart: 1 -> 0, of which waited for: 1 -> 0; matrix products, arithmetic and copies ran while one was open for 1% -> 0% of each run, Pallas kernels for 0% -> 0%
where the time goes in v1:
time: 121 us
  Pallas kernels  99.5 us (82%)
  local copies, waits for them, and re-layouts  20.7 us (17%)
    pallas_call x1, Pallas kernels, body(): fused(boards, history_mask.T, kernels, norm_params, norm_momenta, left_st...  92.5 us
    unnamed x12, local copies, waits for them, and re-layouts  20.7 us
    pallas_call x1, Pallas kernels, body(): finish(*held)  6.98 us

profile of v1, /device:TPU:0, one launch (start us, length us, event | category | flops | bytes accessed | tf_op | source)
XLA Modules:
  0.0 121.1 jit_solution(17127804944770527734)
XLA Ops:
  0.6 92.5 %fused_passes.1 = (f32[2,2304,256]{2,1,0:T(8,128)S(1)}, f32[2,576,2304]{2,1,0:T(8,128)S(1)}, f32[2,576,2304]{2,1,0:T(8,128)S(1)}, f32[2,256,256]{2,1,0:T(8,128)S...) custom-call(f32[12,8,8,256]{3,2,1,0:T(8,128)} %boards.1, ...), custom_call_target="tpu_custom_call" | custom-call | tf_op jit(solution)/shard_map/fused_passes/pallas_call | solution.py:685
  93.2 0.0 copy-start
  93.2 4.1 %copy-done = f32[2,576,2304]{2,1,0:T(8,128)} copy-done((f32[2,576,2304]{2,1,0:T(8,128)}, f32[2,576,2304]{2,1,0:T(8,128)S(1)}, u32[]{:S(2)}) %copy-start) | copy-done | bytes 10616856
  97.3 0.0 copy-start.2
  97.3 4.0 %copy-done.2 = f32[2,576,2304]{2,1,0:T(8,128)} copy-done((f32[2,576,2304]{2,1,0:T(8,128)}, f32[2,576,2304]{2,1,0:T(8,128)S(1)}, u32[]{:S(2)}) %copy-start.2) | copy-done | bytes 10616856
  101.3 0.0 copy-start.4
  101.3 2.2 %copy-done.4 = f32[2,2304,256]{2,1,0:T(8,128)} copy-done((f32[2,2304,256]{2,1,0:T(8,128)}, f32[2,2304,256]{2,1,0:T(8,128)S(1)}, u32[]{:S(2)}) %copy-start.4) | copy-done | bytes 4718616
  103.6 0.0 copy-start.1
  103.6 4.0 %copy-done.1 = f32[2,576,2304]{2,1,0:T(8,128)S(1)} copy-done((f32[2,576,2304]{2,1,0:T(8,128)S(1)}, f32[2,576,2304]{2,1,0:T(8,128)}, u32[]{:S(2)}) %copy-start.1) | copy-done | bytes 10616856
  107.6 0.0 copy-start.3
  107.6 4.0 %copy-done.3 = f32[2,576,2304]{2,1,0:T(8,128)S(1)} copy-done((f32[2,576,2304]{2,1,0:T(8,128)S(1)}, f32[2,576,2304]{2,1,0:T(8,128)}, u32[]{:S(2)}) %copy-start.3) | copy-done | bytes 10616856
  111.6 0.0 copy-start.5
  111.6 2.3 %copy-done.5 = f32[2,2304,256]{2,1,0:T(8,128)S(1)} copy-done((f32[2,2304,256]{2,1,0:T(8,128)S(1)}, f32[2,2304,256]{2,1,0:T(8,128)}, u32[]{:S(2)}) %copy-start.5) | copy-done | bytes 4718616
  113.9 7.0 %finish.1 = (f32[12,8,8,256]{3,2,1,0:T(8,128)}, f32[12,8,8,256]{3,2,1,0:T(8,128)}, f32[2,576,256]{2,1,0:T(8,128)}, f32[2,576,256]{2,1,0:T(8,128)}, f32[2,256,256...) custom-call(f32[2,2304,256]{2,1,0:T(8,128)S(1)} %copy-done.5, ...), custom_call_target="tpu_custom_call" | custom-call | tf_op jit(solution)/shard_map/finish/pallas_call | solution.py:721
Async XLA Ops:
  93.2 4.1 %copy-start = (f32[2,576,2304]{2,1,0:T(8,128)}, f32[2,576,2304]{2,1,0:T(8,128)S(1)}, u32[]{:S(2)}) copy-start(f32[2,576,2304]{2,1,0:T(8,128)S(1)} %get-tuple-element.27.stats) | copy-start | bytes 31850500
  97.3 4.0 %copy-start.2 = (f32[2,576,2304]{2,1,0:T(8,128)}, f32[2,576,2304]{2,1,0:T(8,128)S(1)}, u32[]{:S(2)}) copy-start(f32[2,576,2304]{2,1,0:T(8,128)S(1)} %get-tuple-element.28.roots) | copy-start | bytes 31850500
  101.3 2.2 %copy-start.4 = (f32[2,2304,256]{2,1,0:T(8,128)}, f32[2,2304,256]{2,1,0:T(8,128)S(1)}, u32[]{:S(2)}) copy-start(f32[2,2304,256]{2,1,0:T(8,128)S(1)} %get-tuple-element.26.g_full) | copy-start | bytes 14155780
  103.6 4.0 %copy-start.1 = (f32[2,576,2304]{2,1,0:T(8,128)S(1)}, f32[2,576,2304]{2,1,0:T(8,128)}, u32[]{:S(2)}) copy-start(f32[2,576,2304]{2,1,0:T(8,128)} %copy-done) | copy-start | bytes 31850500
  107.6 4.0 %copy-start.3 = (f32[2,576,2304]{2,1,0:T(8,128)S(1)}, f32[2,576,2304]{2,1,0:T(8,128)}, u32[]{:S(2)}) copy-start(f32[2,576,2304]{2,1,0:T(8,128)} %copy-done.2) | copy-start | bytes 31850500
  111.6 2.3 %copy-start.5 = (f32[2,2304,256]{2,1,0:T(8,128)S(1)}, f32[2,2304,256]{2,1,0:T(8,128)}, u32[]{:S(2)}) copy-start(f32[2,2304,256]{2,1,0:T(8,128)} %copy-done.4) | copy-start | bytes 14155780

commit v2 on v1

--- a/solution.py
+++ b/solution.py
@@ -21,6 +21,23 @@
 F32 = jnp.float32
 BF16 = jnp.bfloat16
 MIB = 2**20
+
+
+PIECES = (
+    (1, 1, "c12z"), (1, 1, "cz12"), (1, 1, "cz12"), (1, 2, "c12ab"),
+    (1, 2, "c12ab"), (1, 1, "c12z"), (1, 1, "c12z"), (0, 1, "c1ab2"),
+    (0, 2, "c12z"), (0, 1, "cab12"), (0, 1, "c12ab"), (0, 3, "c12z"),
+    (0, 1, "c12z"),
+)
+ORDER = (
+    3, -1, -1, -1, -2, 3, 6, 5, 2, 4, 6, 0, 5, 2, 1, 4, 1, 3, 0, -3,
+    6, 9, 7, 10, 12, 5, 9, 7, 11, 4, 8, 3, 0, 10, 6, 12, 5, 2, 7, 11,
+    9, 4, 0, 3, 10, 12, 7, 8, 5, -4, 4, 6, 11, 2, 10, 12, 3, 1, 0, 7,
+    9, 8, 10, 5, 4, 11, 9, 6, 7, 3, 1, 2, 12, 5, 9, 0, 10, 4, 6, 7,
+    1, 8, 3, 2, 9, 0, 11, -4, 12, 4, 10, 6, 3, 1, 9, 7, 8, 12, 10, 4,
+    2, 0, 11, -4, 1, 7, 0, 10, 8, 9, 11, 4, 3, 4, 8, 9, 5, 2, 10, 9,
+    12, 1, 10, 11, 3, 2, 7, 8, 5, 6, 1, 12, 11, -5, 7, 8,
+)
 
 
 def dot(lhs, rhs, lhs_dim, rhs_dim):
@@ -90,11 +107,7 @@
     d_hid,
     gp,
     red,
-    half_in,
-    first_in,
-    second_in,
-    depth_in,
-    more_in,
+    arrived,
     load_sem,
     red_send,
     red_recv,
@@ -105,9 +118,7 @@
     line = pos * SIDE
     rows = line * SIDE
     count = float(rows * nw * nn)
-    taps = 9 * chan
     chunk = 3 * chan
-    part0, part1, part2, part3 = chunk // 2, chunk // 4, chunk // 8, chunk // 32
     wide, narrow = lax.axis_index("wide"), lax.axis_index("narrow")
     me = wide * nn + narrow
     extra_bits = list(range(3, nw.bit_length() - 1))
@@ -117,7 +128,7 @@
         copy.start()
         return copy
 
-    got_k0 = load(0, kernels.at[0], kf.at[0])
+    got_k0 = load(0, kernels.at[0], kf)
     got_mask = load(1, mask_t, mk)
     got_boards = [load(2 + i, boards.at[:, i], bd.at[i]) for i in range(SIDE)]
     got_par = load(10, params, par)
@@ -214,44 +225,53 @@
             for a in range(3)
         )
 
-    def conv_back(grid, k):
+    def conv_back(grid, k, a):
         result = None
-        for a in range(3):
-            for b in range(3):
-                tap = 3 * (2 - a) + (2 - b)
-                term = dot(
-                    grid[a * line : a * line + rows, b * chan : (b + 1) * chan],
-                    wb[k, :, tap * chan : (tap + 1) * chan],
-                    1,
-                    0,
-                )
-                result = term if result is None else result + term
+        for b in range(3):
+            tap = 3 * (2 - a) + (2 - b)
+            term = dot(
+                grid[a * line : a * line + rows, b * chan : (b + 1) * chan],
+                wb[k, :, tap * chan : (tap + 1) * chan],
+                1,
+                0,
+            )
+            result = term if result is None else result + term
         return result
 
     core = bit_of(narrow, 0)
     x_bit, y_bit = bit_of(narrow, 1), bit_of(wide, 0)
     z_low, z_high = bit_of(wide, 1), bit_of(wide, 2)
     z_pos = z_low + 2 * z_high
-    core_dev = (wide, flip(narrow, 0))
     x_dev = (wide, flip(narrow, 1))
     y_dev = (flip(wide, 0), narrow)
-    first_dev = (pick(core, y_dev[0], x_dev[0]), pick(core, y_dev[1], x_dev[1]))
-    second_dev = (pick(core, x_dev[0], y_dev[0]), pick(core, x_dev[1], y_dev[1]))
-    first_bit, second_bit = pick(core, y_bit, x_bit), pick(core, x_bit, y_bit)
-
-    def z_other(q):
-        low = 1 - z_low if q & 1 else z_low
-        high = 1 - z_high if q & 2 else z_high
-        return low + 2 * high
-
-    sends = []
-
-    def remote(k, a, slot, src, dst, dev):
+    pairs = {
+        "c": ((wide, flip(narrow, 0)), core),
+        "1": (
+            (pick(core, y_dev[0], x_dev[0]), pick(core, y_dev[1], x_dev[1])),
+            pick(core, y_bit, x_bit),
+        ),
+        "2": (
+            (pick(core, x_dev[0], y_dev[0]), pick(core, x_dev[1], y_dev[1])),
+            pick(core, x_bit, y_bit),
+        ),
+        "a": ((flip(wide, 1), narrow), z_low),
+        "b": ((flip(wide, 2), narrow), z_high),
+    }
+    line_devs = []
+    for q in (3, 2, 1):
+        other = (1 - z_low if q & 1 else z_low) + 2 * (1 - z_high if q & 2 else z_high)
+        line_devs.append((other, (wide + 2 * (other - z_pos), narrow)))
+
+    sends, done = [], []
+    filled = [0, 0]
+
+    def remote(src, dst, dev):
+        slot = len(sends)
         copy = pltpu.make_async_remote_copy(
             src_ref=src,
             dst_ref=dst,
-            send_sem=g_send.at[k, a, slot],
-            recv_sem=g_recv.at[k, a, slot],
+            send_sem=g_send.at[slot],
+            recv_sem=g_recv.at[slot],
             device_id=dev,
             device_id_type=MESH,
         )
@@ -259,104 +279,82 @@
         sends.append(copy)
         return copy
 
-    def exchange(k, a):
-        base = a * chunk
-        off0 = base + core * part0
-        off1 = off0 + first_bit * part1
-        off2 = off1 + second_bit * part2
-        off3 = off2 + z_pos * part3
-        live = {}
-
-        def at(start, size):
-            return pl.ds(pl.multiple_of(start, 8), size)
-
-        def begin():
-            src = gp.at[k, at(base + (1 - core) * part0, part0)]
-            live["c"] = remote(k, a, 0, src, half_in.at[k, a], core_dev)
-
-        def after_core():
-            live["c"].wait_recv()
-            own = at(off0, part0)
-            gp[k, own] = gp[k, own] + half_in[k, a]
-            src = gp.at[k, at(off0 + (1 - first_bit) * part1, part1)]
-            live["1"] = remote(k, a, 1, src, first_in.at[k, a], first_dev)
-
-        def after_first():
-            live["1"].wait_recv()
-            own = at(off1, part1)
-            gp[k, own] = gp[k, own] + first_in[k, a]
-            src = gp.at[k, at(off1 + (1 - second_bit) * part2, part2)]
-            live["2"] = remote(k, a, 2, src, second_in.at[k, a], second_dev)
-
-        def after_second():
-            live["2"].wait_recv()
-            own = at(off2, part2)
-            gp[k, own] = gp[k, own] + second_in[k, a]
-            live["z"] = []
-            for q in (3, 2, 1):
-                other = z_other(q)
-                dev = (wide + 2 * (other - z_pos), narrow)
-                src = gp.at[k, at(off2 + other * part3, part3)]
-                live["z"].append(remote(k, a, 2 + q, src, depth_in.at[k, a, q - 1], dev))
-
-        def after_depth():
-            for copy in live["z"]:
+    def at(start, size):
+        return pl.ds(pl.multiple_of(start, 8), size)
+
+    def take(k, size):
+        start = filled[k]
+        filled[k] += size
+        return pl.ds(start, size)
+
+    def piece(k, base, size, kind, compute):
+        starts, sizes, live = [base], [size], {}
+        for step in kind:
+            place = z_pos if step == "z" else pairs[step][1]
+            sizes.append(sizes[-1] // (4 if step == "z" else 2))
+            starts.append(starts[-1] + place * sizes[-1])
+        last = len(kind) - 1
+        own = at(starts[-1], sizes[-1])
+
+        def scatter(i):
+            part = sizes[i + 1]
+            if kind[i] == "z":
+                targets = line_devs
+            else:
+                dev, place = pairs[kind[i]]
+                targets = [(1 - place, dev)]
+            live[i] = []
+            for place, dev in targets:
+                into = take(k, part)
+                src = gp.at[k, at(starts[i] + place * part, part)]
+                live[i].append((remote(src, arrived.at[k, into], dev), into))
+
+        def add(i):
+            rows_here = at(starts[i + 1], sizes[i + 1])
+            value = gp[k, rows_here]
+            for copy, into in live[i]:
                 copy.wait_recv()
-            own = at(off3, part3)
-            value = ((gp[k, own] + depth_in[k, a, 0]) + depth_in[k, a, 1]) + depth_in[k, a, 2]
-            for e, b in enumerate(extra_bits):
+                value = value + arrived[k, into]
+            return rows_here, value
+
+        def gather(i):
+            ref = g_full.at[k, at(starts[i + 1], sizes[i + 1])]
+            targets = line_devs if kind[i] == "z" else [(0, pairs[kind[i]][0])]
+            live[i] = [remote(ref, ref, dev) for _, dev in targets]
+
+        def start():
+            compute()
+            scatter(0)
+
+        def middle(i):
+            rows_here, value = add(i)
+            gp[k, rows_here] = value
+            scatter(i + 1)
+
+        def turn():
+            _, value = add(last)
+            for b in extra_bits:
                 gp[k, own] = value
-                copy = remote(
-                    k, a, 12 + e, gp.at[k, own], more_in.at[k, a, e], (flip(wide, b), narrow)
-                )
+                into = take(k, sizes[-1])
+                copy = remote(gp.at[k, own], arrived.at[k, into], (flip(wide, b), narrow))
+                copy.wait()
+                done.append(copy)
+                value = value + arrived[k, into]
+            g_full[k, own] = value * (1.0 / count)
+            gather(last)
+
+        def back(i):
+            for copy in live[i]:
                 copy.wait_recv()
-                copy.wait_send()
-                sends.pop()
-                value = value + more_in[k, a, e]
-            g_full[k, own] = value * (1.0 / count)
-            live["gz"] = []
-            for q in (3, 2, 1):
-                dev = (wide + 2 * (z_other(q) - z_pos), narrow)
-                live["gz"].append(
-                    remote(k, a, 5 + q, g_full.at[k, own], g_full.at[k, own], dev)
-                )
-
-        def back_depth():
-            for copy in live["gz"]:
-                copy.wait_recv()
-            ref = g_full.at[k, at(off2, part2)]
-            live["g2"] = remote(k, a, 9, ref, ref, second_dev)
-
-        def back_second():
-            live["g2"].wait_recv()
-            ref = g_full.at[k, at(off1, part1)]
-            live["g1"] = remote(k, a, 10, ref, ref, first_dev)
-
-        def back_first():
-            live["g1"].wait_recv()
-            ref = g_full.at[k, at(off0, part0)]
-            live["gc"] = remote(k, a, 11, ref, ref, core_dev)
-
-        def end():
-            live["gc"].wait_recv()
-
-        return [
-            begin,
-            after_core,
-            after_first,
-            after_second,
-            after_depth,
-            back_depth,
-            back_second,
-            back_first,
-            end,
-        ]
-
-    events = {(k, a): exchange(k, a) for k in range(2) for a in range(3)}
-
-    def do(k, step):
-        for a in range(3):
-            events[k, a][step]()
+            if i:
+                gather(i - 1)
+
+        return (
+            [start]
+            + [functools.partial(middle, i) for i in range(last)]
+            + [turn]
+            + [functools.partial(back, i) for i in range(last, -1, -1)]
+        )
 
     empty = jnp.zeros((line, 3 * chan), BF16)
     for grid in (x_one, x_two, dgrid):
@@ -376,8 +374,7 @@
     planes = dot(by_row, spread_chan, 0, 0)
 
     got_k0.wait()
-    wb[0] = kf[0].astype(BF16)
-    got_k1 = load(11, kernels.at[1], kf.at[1])
+    wb[0] = kf[...].astype(BF16)
     got_ct = [load(12 + i, cotangent.at[:, i], ct.at[i]) for i in range(SIDE)]
     for i in range(SIDE):
         got_boards[i].wait()
@@ -391,6 +388,17 @@
     share(0, local)
 
     got_par.wait()
+
+    def keep_share(k):
+        share_width = kt.shape[1]
+        span = ktmp.shape[0]
+        start = narrow * share_width
+        block = (start // 128) * 128
+        ktmp[...] = kf[:, pl.ds(pl.multiple_of(block, 128), span)].T
+        kt[k] = ktmp[pl.ds(pl.multiple_of(start - block, 8), share_width), :]
+
+    keep_share(0)
+    got_k1 = load(11, kernels.at[1], kf)
     late = [
         load(20, momenta, mom),
         load(21, left_stats, lstats_v),
@@ -399,17 +407,7 @@
         load(24, right_stats, stats_v),
     ]
     got_k1.wait()
-    wb[1] = kf[1].astype(BF16)
-
-    def keep_share(k):
-        share_width = kt.shape[1]
-        span = ktmp.shape[0]
-        start = narrow * share_width
-        block = (start // 128) * 128
-        ktmp[...] = kf[k, :, pl.ds(pl.multiple_of(block, 128), span)].T
-        kt[k] = ktmp[pl.ds(pl.multiple_of(start - block, 8), share_width), :]
-
-    keep_share(0)
+    wb[1] = kf[...].astype(BF16)
     keep_share(1)
 
     gain_one, shift_one = par[0, 0:1, :], par[0, 1:2, :]
@@ -474,41 +472,67 @@
         lost = (shift_two_sum + h_two[at, :] * gain_two_sum) * (1.0 / count)
         put_shifted(dgrid, i, scale_two * (d_sum[at, :] - lost))
 
-    def weight_chunk(grid, k, a):
-        gp[k, a * chunk : (a + 1) * chunk, :] = dot(
-            grid[a * line : a * line + rows, :], dgrid[line : line + rows, chan : 2 * chan], 0, 0
-        )
-        events[k, a][0]()
-
-    for a in range(3):
-        weight_chunk(x_two, 1, a)
-    d_hid[...] = conv_back(dgrid, 1)
-    do(1, 1)
-
-    def pre_line(i, carry):
-        at = at_line(i)
-        d_pre = d_hid[at, :] * slope_one[at, :]
-        d_hid[at, :] = d_pre
-        return carry[0] + fold(d_pre * h_one[at, :]), carry[1] + fold(d_pre)
-
-    share(3, close(*lax.fori_loop(0, SIDE, pre_line, (nothing, nothing))))
-    gain_one_sum, shift_one_sum = totals(3)
-    scale_one = gain_one * inv_one
-
-    @pl.loop(0, SIDE)
-    def _(i):
-        at = at_line(i)
-        lost = (shift_one_sum + h_one[at, :] * gain_one_sum) * (1.0 / count)
-        put_shifted(dgrid, i, scale_one * (d_hid[at, :] - lost))
-
-    for a in range(3):
-        weight_chunk(x_one, 0, a)
-    do(1, 2)
-    d_hid[...] = conv_back(dgrid, 0)
-    do(0, 1)
-    for i in range(SIDE):
-        at = at_line(i)
-        bg[i] = ((d_sum[at, :] + d_hid[at, :]) * planes).reshape(pos, SIDE, chan)
+    def weights(k, first, taps_here):
+        grid = (x_one, x_two)[k]
+        tap = first
+        while tap < first + taps_here:
+            a, b = divmod(tap, 3)
+            n = min(3 - b, first + taps_here - tap)
+            g_part = dot(
+                grid[a * line : a * line + rows, b * chan : (b + n) * chan],
+                dgrid[line : line + rows, chan : 2 * chan],
+                0,
+                0,
+            )
+            gp[k, tap * chan : (tap + n) * chan, :] = g_part
+            tap += n
+
+    def add_back(k, a):
+        term = conv_back(dgrid, k, a)
+        d_hid[...] = d_hid[...] + term if a else term
+
+    kept = {}
+
+    def pre_sums():
+        def pre_line(i, carry):
+            at = at_line(i)
+            d_pre = d_hid[at, :] * slope_one[at, :]
+            d_hid[at, :] = d_pre
+            return carry[0] + fold(d_pre * h_one[at, :]), carry[1] + fold(d_pre)
+
+        share(3, close(*lax.fori_loop(0, SIDE, pre_line, (nothing, nothing))))
+
+    def first_conv_grad():
+        kept["sums"] = gain_one_sum, shift_one_sum = totals(3)
+        scale_one = gain_one * inv_one
+
+        @pl.loop(0, SIDE)
+        def _(i):
+            at = at_line(i)
+            lost = (shift_one_sum + h_one[at, :] * gain_one_sum) * (1.0 / count)
+            put_shifted(dgrid, i, scale_one * (d_hid[at, :] - lost))
+
+    def board_grads():
+        for i in range(SIDE):
+            at = at_line(i)
+            bg[i] = ((d_sum[at, :] + d_hid[at, :]) * planes).reshape(pos, SIDE, chan)
+
+    steps = []
+    tap_at = [0, 0]
+    for k, n, kind in PIECES:
+        compute = functools.partial(weights, k, tap_at[k], n)
+        steps.append(iter(piece(k, tap_at[k] * chan, n * chan, kind, compute)))
+        tap_at[k] += n
+    passes = {
+        -1: iter([functools.partial(add_back, 1, a) for a in range(3)]),
+        -2: iter([pre_sums]),
+        -3: iter([first_conv_grad]),
+        -4: iter([functools.partial(add_back, 0, a) for a in range(3)]),
+        -5: iter([board_grads]),
+    }
+    for item in ORDER:
+        next(steps[item] if item >= 0 else passes[item])()
+    gain_one_sum, shift_one_sum = kept["sums"]
 
     for copy in late:
         copy.wait()
@@ -521,21 +545,9 @@
         new_momenta[k] = value
         new_params[k] = par[k] - NORM_RATE * value
 
-    do(1, 3)
-    do(0, 2)
-    do(1, 4)
-    do(0, 3)
-    do(1, 5)
-    do(0, 4)
-    do(1, 6)
-    do(0, 5)
-    do(1, 7)
-    do(0, 6)
-    do(1, 8)
-    do(0, 7)
-    do(0, 8)
     for copy in sends:
-        copy.wait_send()
+        if not any(copy is other for other in done):
+            copy.wait_send()
 
 
 def finish_kernel(
@@ -602,6 +614,14 @@
         copy.wait()
 
 
+def room_of(size, kind, extra):
+    rows = 0
+    for step in kind:
+        size //= 4 if step == "z" else 2
+        rows += 3 * size if step == "z" else size
+    return rows + extra * size
+
+
 def body(
     nw,
     nn,
@@ -642,6 +662,12 @@
         (2, 2, chan),
         (2, 2, chan),
     ]
+    arrivals = max(
+        sum(room_of(n * chan, kind, extra) for layer, n, kind in PIECES if layer == k)
+        for k in range(2)
+    )
+    transfers = sum(2 * len(kind) + 4 * kind.count("z") + extra for _, _, kind in PIECES)
+    room = (49 + extra) * MIB // 2 + (ndev - 32) * 8 * chan * 4 + 8 * chan * max(arrivals - kin, 0)
     fused = pl.pallas_call(
         functools.partial(fused_kernel, dims),
         out_shape=[pltpu.VMEM(shape, F32) for shape in kept],
@@ -653,7 +679,7 @@
             pltpu.VMEM(history_mask.shape[::-1], jnp.int32),
             pltpu.VMEM((2, 2, chan), F32),
             pltpu.VMEM((2, 2, chan), F32),
-            pltpu.VMEM((2, chan, kin), F32),
+            pltpu.VMEM((chan, kin), F32),
             pltpu.VMEM((2, chan, kin), BF16),
             pltpu.VMEM((span, chan), F32),
             pltpu.VMEM((rows + 2 * line, chunk), BF16),
@@ -666,23 +692,19 @@
             pltpu.VMEM((rows, chan), F32),
             pltpu.VMEM((2, kin, chan), F32),
             pltpu.VMEM((4, ndev, 2, chan), F32),
-            pltpu.VMEM((2, 3, chunk // 2, chan), F32),
-            pltpu.VMEM((2, 3, chunk // 4, chan), F32),
-            pltpu.VMEM((2, 3, chunk // 8, chan), F32),
-            pltpu.VMEM((2, 3, 3, chunk // 32, chan), F32),
-            pltpu.VMEM((2, 3, max(extra, 1), chunk // 32, chan), F32),
+            pltpu.VMEM((2, arrivals, chan), F32),
             pltpu.SemaphoreType.DMA((25,)),
             pltpu.SemaphoreType.DMA((4,)),
             pltpu.SemaphoreType.DMA((4,)),
-            pltpu.SemaphoreType.DMA((2, 3, 12 + extra)),
-            pltpu.SemaphoreType.DMA((2, 3, 12 + extra)),
+            pltpu.SemaphoreType.DMA((transfers,)),
+            pltpu.SemaphoreType.DMA((transfers,)),
         ],
         compiler_params=pltpu.CompilerParams(
-            collective_id=0, has_side_effects=True, vmem_limit_bytes=34 * MIB
+            collective_id=0, has_side_effects=True, vmem_limit_bytes=room
         ),
         name="fused_passes",
     )
-    held = fused(
+    given = (
         boards,
         history_mask.T,
         kernels,
@@ -694,6 +716,8 @@
         jnp.swapaxes(right_roots, 1, 2),
         out_cotangent,
     )
+    held = fused(*(pltpu.with_memory_space_constraint(v, pltpu.HBM) for v in given))
+    held = [pltpu.with_memory_space_constraint(v, pltpu.VMEM) for v in held]
     finish = pl.pallas_call(
         functools.partial(finish_kernel, dims),
         out_shape=[
@@ -715,7 +739,7 @@
             pltpu.VMEM((2, chan, chan), F32),
             pltpu.SemaphoreType.DMA((32,)),
         ],
-        compiler_params=pltpu.CompilerParams(vmem_limit_bytes=24 * MIB),
+        compiler_params=pltpu.CompilerParams(vmem_limit_bytes=20 * MIB),
         name="finish",
     )
     block_out, board_grad, grad, kernel, left, right, momenta, params = finish(*held)

time: 121 us -> 82.4 us (0.68)
  local copies, waits for them, and re-layouts: 20.7 us -> 0 us
  Pallas kernels: 99.5 us -> 81.3 us
    unnamed x12 -> x0, local copies, waits for them, and re-layouts: 20.7 us -> none
    pallas_call x1, Pallas kernels: 92.5 us -> 74.2 us  [body(): fused(*(pltpu.with_memory_space_constraint(v, pltpu.HBM) for v in given))]
where the time goes in v2:
time: 82.4 us; the launch traced here: 82.1 us
  Pallas kernels  81.3 us (99%)
    pallas_call x1, Pallas kernels, body(): fused(*(pltpu.with_memory_space_constraint(v, pltpu.HBM) for v in given))  74.2 us
    pallas_call x1, Pallas kernels, body(): finish(*held)  7.16 us

profile of v2, /device:TPU:0, one launch (start us, length us, event | category | flops | bytes accessed | tf_op | source)
XLA Modules:
  0.0 82.1 jit_solution(4708143529081974167)
XLA Ops:
  0.6 74.2 %fused_passes.1 = (f32[2,2304,256]{2,1,0:T(8,128)S(1)}, f32[2,576,2304]{2,1,0:T(8,128)S(1)}, f32[2,576,2304]{2,1,0:T(8,128)S(1)}, f32[2,256,256]{2,1,0:T(8,128)S...) custom-call(f32[12,8,8,256]{3,2,1,0:T(8,128)} %boards.1, ...), custom_call_target="tpu_custom_call" | custom-call | tf_op jit(solution)/shard_map/fused_passes/pallas_call | solution.py:719
  74.8 7.2 %finish.1 = (f32[12,8,8,256]{3,2,1,0:T(8,128)}, f32[12,8,8,256]{3,2,1,0:T(8,128)}, f32[2,576,256]{2,1,0:T(8,128)}, f32[2,576,256]{2,1,0:T(8,128)}, f32[2,256,256...) custom-call(f32[2,2304,256]{2,1,0:T(8,128)S(1)} %get-tuple-element.26.g_full, ...), custom_call_target="tpu_custom_call" | custom-call | tf_op jit(solution)/shard_map/finish/pallas_call | solution.py:745

commit v3 on v2

--- a/solution.py
+++ b/solution.py
@@ -24,19 +24,21 @@
 
 
 PIECES = (
-    (1, 1, "c12z"), (1, 1, "cz12"), (1, 1, "cz12"), (1, 2, "c12ab"),
-    (1, 2, "c12ab"), (1, 1, "c12z"), (1, 1, "c12z"), (0, 1, "c1ab2"),
-    (0, 2, "c12z"), (0, 1, "cab12"), (0, 1, "c12ab"), (0, 3, "c12z"),
-    (0, 1, "c12z"),
+    (1, 1, "c12z"), (1, 1, "cz12"), (1, 1, "c12ab"), (1, 1, "cab12"),
+    (1, 1, "c12ab"), (1, 2, "c12z"), (1, 1, "c12ab"), (1, 1, "c12z"),
+    (0, 1, "c12ab"), (0, 1, "c12z"), (0, 1, "c12z"), (0, 1, "c12ab"),
+    (0, 1, "c12z"), (0, 2, "c12ab"), (0, 1, "c12z"), (0, 1, "cab12"),
 )
 ORDER = (
-    3, -1, -1, -1, -2, 3, 6, 5, 2, 4, 6, 0, 5, 2, 1, 4, 1, 3, 0, -3,
-    6, 9, 7, 10, 12, 5, 9, 7, 11, 4, 8, 3, 0, 10, 6, 12, 5, 2, 7, 11,
-    9, 4, 0, 3, 10, 12, 7, 8, 5, -4, 4, 6, 11, 2, 10, 12, 3, 1, 0, 7,
-    9, 8, 10, 5, 4, 11, 9, 6, 7, 3, 1, 2, 12, 5, 9, 0, 10, 4, 6, 7,
-    1, 8, 3, 2, 9, 0, 11, -4, 12, 4, 10, 6, 3, 1, 9, 7, 8, 12, 10, 4,
-    2, 0, 11, -4, 1, 7, 0, 10, 8, 9, 11, 4, 3, 4, 8, 9, 5, 2, 10, 9,
-    12, 1, 10, 11, 3, 2, 7, 8, 5, 6, 1, 12, 11, -5, 7, 8,
+    2, 6, 5, -1, 3, 2, -1, 6, -1, -2, 3, 5, 7, 1, 0, 4, 7, 4, 2, 1,
+    6, 3, 5, 0, -3, 8, 15, 13, 7, 2, 4, 6, 8, 15, 12, 10, 13, 5, 0, -4,
+    1, 12, 7, 11, 2, 9, 3, 4, 6, 8, 14, 11, 10, 15, 13, 0, 12, 9, 1, 4,
+    8, 2, 6, 3, 7, 11, 5, 14, 10, 13, 15, 12, 9, 4, 8, 11, 3, 2, 6, 0,
+    1, 14, 10, 15, 13, 7, 9, 5, -4, 1, 8, 4, 11, 12, 2, 15, 3, 6, 7, 14,
+    0, 13, 10, 5, -4, 4, 8, 9, 11, 15, 3, 2, 12, 0, -5, 13, 6, 14, 8, 15,
+    5, 4, 11, 10, 12, 7, 1, 9, 3, 13, 8, 14, 11, 0, 10, 2, 15, 4, 9, 12,
+    6, 13, 12, 7, 14, 6, 8, 11, 0, 3, 5, 1, 10, 9, 8, 3, 2, 4, 15, 1,
+    -7, -7, 13, 14, -7, 11, -7, 10, 15, 14, 9, 13, 11,
 )
 
 
@@ -96,7 +98,6 @@
     mom,
     kf,
     wb,
-    ktmp,
     x_one,
     x_two,
     dgrid,
@@ -128,10 +129,14 @@
         copy.start()
         return copy
 
-    got_k0 = load(0, kernels.at[0], kf)
-    got_mask = load(1, mask_t, mk)
-    got_boards = [load(2 + i, boards.at[:, i], bd.at[i]) for i in range(SIDE)]
-    got_par = load(10, params, par)
+    got_mask = load(0, mask_t, mk)
+    for i in range(SIDE):
+        load(1, boards.at[:, i], bd.at[i])
+    got_k0 = [
+        load(9 + a, kernels.at[0, :, pl.ds(a * chunk, chunk)], kf.at[:, pl.ds(a * chunk, chunk)])
+        for a in range(3)
+    ]
+    got_par = load(3, params, par)
 
     def each_other(act):
         if nw * nn <= 32:
@@ -163,8 +168,8 @@
             pltpu.make_async_remote_copy(
                 src_ref=red.at[slot, me],
                 dst_ref=red.at[slot, me],
-                send_sem=red_send.at[slot],
-                recv_sem=red_recv.at[slot],
+                send_sem=red_send.at[0],
+                recv_sem=red_recv.at[slot % 2],
                 device_id=dev,
                 device_id_type=MESH,
             ).start()
@@ -173,8 +178,8 @@
 
     def collect(slot):
         others = red.at[slot, pl.ds(0, nw * nn - 1)]
-        pltpu.make_async_copy(others, others, red_recv.at[slot]).wait()
-        pltpu.make_async_copy(others, others, red_send.at[slot]).wait()
+        pltpu.make_async_copy(others, others, red_recv.at[slot % 2]).wait()
+        pltpu.make_async_copy(others, others, red_send.at[0]).wait()
         return red[slot]
 
     def moments(slot):
@@ -214,16 +219,20 @@
     def at_line(i):
         return pl.ds(pl.multiple_of(i * line, 8), line)
 
-    def conv(grid, k):
-        return sum(
-            dot(
-                grid[a * line : a * line + rows, :],
-                wb[k, :, a * chunk : (a + 1) * chunk],
-                1,
-                1,
+    def conv(grid, k, result):
+        tile = rows // 2
+
+        @pl.loop(0, 2)
+        def _(i):
+            result[pl.ds(pl.multiple_of(i * tile, 8), tile), :] = sum(
+                dot(
+                    grid[pl.ds(pl.multiple_of(a * line + i * tile, 16), tile), :],
+                    wb[k, :, a * chunk : (a + 1) * chunk],
+                    1,
+                    1,
+                )
+                for a in range(3)
             )
-            for a in range(3)
-        )
 
     def conv_back(grid, k, a):
         result = None
@@ -262,39 +271,38 @@
         other = (1 - z_low if q & 1 else z_low) + 2 * (1 - z_high if q & 2 else z_high)
         line_devs.append((other, (wide + 2 * (other - z_pos), narrow)))
 
-    sends, done = [], []
     filled = [0, 0]
-
-    def remote(src, dst, dev):
-        slot = len(sends)
-        copy = pltpu.make_async_remote_copy(
+    flags = iter(range(g_recv.shape[0]))
+    sent = []
+
+    def remote(src, dst, dev, send_sem, recv_sem):
+        pltpu.make_async_remote_copy(
             src_ref=src,
             dst_ref=dst,
-            send_sem=g_send.at[slot],
-            recv_sem=g_recv.at[slot],
+            send_sem=send_sem,
+            recv_sem=recv_sem,
             device_id=dev,
             device_id_type=MESH,
-        )
-        copy.start()
-        sends.append(copy)
-        return copy
+        ).start()
+
+    def wait_for(ref, sem):
+        pltpu.make_async_copy(ref, ref, sem).wait()
 
     def at(start, size):
         return pl.ds(pl.multiple_of(start, 8), size)
 
-    def take(k, size):
-        start = filled[k]
-        filled[k] += size
-        return pl.ds(start, size)
-
     def piece(k, base, size, kind, compute):
-        starts, sizes, live = [base], [size], {}
+        starts, sizes, into = [base], [size], []
         for step in kind:
             place = z_pos if step == "z" else pairs[step][1]
             sizes.append(sizes[-1] // (4 if step == "z" else 2))
             starts.append(starts[-1] + place * sizes[-1])
         last = len(kind) - 1
         own = at(starts[-1], sizes[-1])
+        flag = [g_recv.at[next(flags)] for _ in kind]
+        back_flag = [g_recv.at[next(flags)]] + flag[:-1]
+        out_flag = g_send.at[len(sent)]
+        sent.append((k, 2 * (size - sizes[-1]), out_flag))
 
         def scatter(i):
             part = sizes[i + 1]
@@ -303,24 +311,29 @@
             else:
                 dev, place = pairs[kind[i]]
                 targets = [(1 - place, dev)]
-            live[i] = []
-            for place, dev in targets:
-                into = take(k, part)
+            start = filled[k]
+            into.append((start, part * len(targets)))
+            filled[k] += part * len(targets)
+            for q, (place, dev) in enumerate(targets):
                 src = gp.at[k, at(starts[i] + place * part, part)]
-                live[i].append((remote(src, arrived.at[k, into], dev), into))
+                dst = arrived.at[k, pl.ds(start + q * part, part)]
+                remote(src, dst, dev, out_flag, flag[i])
 
         def add(i):
-            rows_here = at(starts[i + 1], sizes[i + 1])
+            part = sizes[i + 1]
+            start, total = into[i]
+            wait_for(arrived.at[k, pl.ds(start, total)], flag[i])
+            rows_here = at(starts[i + 1], part)
             value = gp[k, rows_here]
-            for copy, into in live[i]:
-                copy.wait_recv()
-                value = value + arrived[k, into]
+            for q in range(total // part):
+                value = value + arrived[k, start + q * part : start + (q + 1) * part]
             return rows_here, value
 
         def gather(i):
             ref = g_full.at[k, at(starts[i + 1], sizes[i + 1])]
             targets = line_devs if kind[i] == "z" else [(0, pairs[kind[i]][0])]
-            live[i] = [remote(ref, ref, dev) for _, dev in targets]
+            for _, dev in targets:
+                remote(ref, ref, dev, out_flag, back_flag[i])
 
         def start():
             compute()
@@ -335,17 +348,19 @@
             _, value = add(last)
             for b in extra_bits:
                 gp[k, own] = value
-                into = take(k, sizes[-1])
-                copy = remote(gp.at[k, own], arrived.at[k, into], (flip(wide, b), narrow))
-                copy.wait()
-                done.append(copy)
-                value = value + arrived[k, into]
+                into_more = arrived.at[k, pl.ds(filled[k], sizes[-1])]
+                more = g_recv.at[next(flags)], g_recv.at[next(flags)]
+                remote(gp.at[k, own], into_more, (flip(wide, b), narrow), *more)
+                wait_for(into_more, more[0])
+                wait_for(into_more, more[1])
+                value = value + arrived[k, filled[k] : filled[k] + sizes[-1]]
+                filled[k] += sizes[-1]
             g_full[k, own] = value * (1.0 / count)
             gather(last)
 
         def back(i):
-            for copy in live[i]:
-                copy.wait_recv()
+            got = (3 if kind[i] == "z" else 1) * sizes[i + 1]
+            wait_for(g_full.at[k, pl.ds(base, got)], back_flag[i])
             if i:
                 gather(i - 1)
 
@@ -356,11 +371,12 @@
             + [functools.partial(back, i) for i in range(last, -1, -1)]
         )
 
-    empty = jnp.zeros((line, 3 * chan), BF16)
-    for grid in (x_one, x_two, dgrid):
+    def clear_ends(grid):
+        empty = jnp.zeros((line, 3 * chan), BF16)
         grid[0:line, :] = empty
         grid[line + rows : 2 * line + rows, :] = empty
 
+    clear_ends(x_one)
     got_mask.wait()
     hist = mk.shape[0]
     width = chan // hist
@@ -373,16 +389,17 @@
     by_row = dot(mk[...].astype(F32).astype(BF16), spread_pos, 1, 0).astype(BF16)
     planes = dot(by_row, spread_chan, 0, 0)
 
-    got_k0.wait()
-    wb[0] = kf[...].astype(BF16)
-    got_ct = [load(12 + i, cotangent.at[:, i], ct.at[i]) for i in range(SIDE)]
+    pltpu.make_async_copy(bd, bd, load_sem.at[1]).wait()
     for i in range(SIDE):
-        got_boards[i].wait()
         value = bd[i].reshape(line, chan) * planes
         bd[i] = value.reshape(pos, SIDE, chan)
         put_shifted(x_one, i, value)
 
-    h_one[...] = conv(x_one, 0)
+    for a in range(3):
+        got_k0[a].wait()
+        part = slice(a * chunk, (a + 1) * chunk)
+        wb[0, :, part] = kf[:, part].astype(BF16)
+    conv(x_one, 0, h_one)
     local = local_moments(h_one)
     pl.semaphore_wait(barrier, nw * nn - 1)
     share(0, local)
@@ -391,20 +408,24 @@
 
     def keep_share(k):
         share_width = kt.shape[1]
-        span = ktmp.shape[0]
+        span = -(-(share_width + 64) // 128) * 128
         start = narrow * share_width
         block = (start // 128) * 128
-        ktmp[...] = kf[:, pl.ds(pl.multiple_of(block, 128), span)].T
-        kt[k] = ktmp[pl.ds(pl.multiple_of(start - block, 8), share_width), :]
-
+        d_hid[0:span, :] = kf[:, pl.ds(pl.multiple_of(block, 128), span)].T
+        kt[k] = d_hid[pl.ds(pl.multiple_of(start - block, 8), share_width), :]
+
+    clear_ends(x_two)
+    clear_ends(dgrid)
     keep_share(0)
-    got_k1 = load(11, kernels.at[1], kf)
+    got_k1 = load(4, kernels.at[1], kf)
+    for i in range(SIDE):
+        load(5, cotangent.at[:, i], ct.at[i])
     late = [
-        load(20, momenta, mom),
-        load(21, left_stats, lstats_v),
-        load(22, left_roots, lroots_v),
-        load(23, right_roots, roots_v),
-        load(24, right_stats, stats_v),
+        load(6, momenta, mom),
+        load(7, left_stats, lstats_v),
+        load(8, left_roots, lroots_v),
+        load(12, right_roots, roots_v),
+        load(2, right_stats, stats_v),
     ]
     got_k1.wait()
     wb[1] = kf[...].astype(BF16)
@@ -423,7 +444,7 @@
         pre = normed * gain_one + shift_one
         put_shifted(x_two, i, (0.5 * pre) * (1.0 + gelu_tanh(pre)))
 
-    h_two[...] = conv(x_two, 1)
+    conv(x_two, 1, h_two)
     share(1, local_moments(h_two))
 
     @pl.loop(0, SIDE)
@@ -432,8 +453,7 @@
         pre = h_one[at, :] * gain_one + shift_one
         slope_one[at, :] = gelu_slope(pre, gelu_tanh(pre))
 
-    for copy in got_ct:
-        copy.wait()
+    pltpu.make_async_copy(ct, ct, load_sem.at[5]).wait()
     mean_two, inv_two = moments(1)
 
     def fold(value):
@@ -517,6 +537,38 @@
             at = at_line(i)
             bg[i] = ((d_sum[at, :] + d_hid[at, :]) * planes).reshape(pos, SIDE, chan)
 
+    def second_left():
+        for copy in late:
+            copy.wait()
+        for a in range(3):
+            x_two[0:chunk, a * chan : (a + 1) * chan] = g_full[
+                1, a * chunk : (a + 1) * chunk, :
+            ].astype(BF16)
+        blocks = [x_two[0:chunk, a * chan : (a + 1) * chan] for a in range(3)]
+        term = sum(dot(block, block, 0, 0) for block in blocks)
+        lstats_v[1] = STAT_DECAY * lstats_v[1] + (1.0 - STAT_DECAY) * term
+
+    def second_right(a):
+        width = kt.shape[1]
+        start = pl.multiple_of(narrow * width, 8)
+        own = g_full[1, pl.ds(start, width), :].astype(BF16)
+        cols = slice(a * chunk, (a + 1) * chunk)
+        term = dot(own, x_two[0:chunk, a * chan : (a + 1) * chan], 1, 1)
+        stats_v[1, :, cols] = STAT_DECAY * stats_v[1, :, cols] + (1.0 - STAT_DECAY) * term
+
+    def second_kernel():
+        mixed = sum(
+            dot(
+                roots_v[1, :, a * chunk : (a + 1) * chunk].astype(BF16),
+                x_two[0:chunk, a * chan : (a + 1) * chan],
+                1,
+                0,
+            )
+            for a in range(3)
+        )
+        update = dot(mixed.astype(BF16), lroots_v[1].astype(BF16), 1, 1)
+        kt[1] = kt[1] - KERNEL_RATE * update
+
     steps = []
     tap_at = [0, 0]
     for k, n, kind in PIECES:
@@ -529,13 +581,12 @@
         -3: iter([first_conv_grad]),
         -4: iter([functools.partial(add_back, 0, a) for a in range(3)]),
         -5: iter([board_grads]),
+        -7: iter([second_left, lambda: (second_right(0), second_right(1)), lambda: second_right(2), second_kernel]),
     }
     for item in ORDER:
         next(steps[item] if item >= 0 else passes[item])()
     gain_one_sum, shift_one_sum = kept["sums"]
 
-    for copy in late:
-        copy.wait()
     norm_grad = [
         jnp.concatenate([gain_one_sum, shift_one_sum], axis=0),
         jnp.concatenate([gain_two_sum, shift_two_sum], axis=0),
@@ -545,9 +596,8 @@
         new_momenta[k] = value
         new_params[k] = par[k] - NORM_RATE * value
 
-    for copy in sends:
-        if not any(copy is other for other in done):
-            copy.wait_send()
+    for k, size, out_flag in sent:
+        wait_for(gp.at[k, pl.ds(0, size)], out_flag)
 
 
 def finish_kernel(
@@ -580,38 +630,37 @@
     chunk = 3 * chan
     share_width = kt.shape[1]
     start = pl.multiple_of(lax.axis_index("narrow") * share_width, 8)
-    copies = []
-
-    def put(src, dst):
-        copy = pltpu.make_async_copy(src, dst, sem.at[len(copies)])
-        copy.start()
-        copies.append(copy)
-
+
+    def put(slot, src, dst):
+        pltpu.make_async_copy(src, dst, sem.at[slot]).start()
+
+    put(0, stats.at[1], o_right.at[1])
     for k in range(2):
-        put(g_full.at[k, pl.ds(start, share_width)], o_grad.at[k])
-        gb[k] = g_full[k].astype(BF16)
-        own = g_full[k, pl.ds(start, share_width), :].astype(BF16)
-        for q in range(3):
-            cols = pl.ds(q * chunk, chunk)
-            term = dot(own, gb[k, cols, :], 1, 1)
-            nr[k, q] = STAT_DECAY * stats[k, :, cols] + (1.0 - STAT_DECAY) * term
-            put(nr.at[k, q], o_right.at[k, :, cols])
-        if k == 0:
-            for i in range(SIDE):
-                put(bo.at[i], o_block.at[:, i])
-                put(bg.at[i], o_board.at[:, i])
-            put(momenta, o_momenta)
-            put(params, o_params)
-    for k in range(2):
-        term = dot(gb[k], gb[k], 0, 0)
-        nl[k] = STAT_DECAY * lstats[k] + (1.0 - STAT_DECAY) * term
-        put(nl.at[k], o_left.at[k])
-        mixed = dot(roots[k].astype(BF16), gb[k], 1, 0)
-        update = dot(mixed.astype(BF16), lroots[k].astype(BF16), 1, 1)
-        nk[k] = kt[k] - KERNEL_RATE * update
-        put(nk.at[k], o_kernel.at[k])
-    for copy in copies:
-        copy.wait()
+        put(1, g_full.at[k, pl.ds(start, share_width)], o_grad.at[k])
+    put(2, kt.at[1], o_kernel.at[1])
+    put(3, lstats.at[1], o_left.at[1])
+    for i in range(SIDE):
+        put(4, bo.at[i], o_block.at[:, i])
+        put(5, bg.at[i], o_board.at[:, i])
+    put(6, momenta, o_momenta)
+    put(7, params, o_params)
+    gb[...] = g_full[0].astype(BF16)
+    own = g_full[0, pl.ds(start, share_width), :].astype(BF16)
+    for q in range(3):
+        cols = pl.ds(q * chunk, chunk)
+        term = dot(own, gb[cols, :], 1, 1)
+        nr[q] = STAT_DECAY * stats[0, :, cols] + (1.0 - STAT_DECAY) * term
+        put(8, nr.at[q], o_right.at[0, :, cols])
+    term = dot(gb[...], gb[...], 0, 0)
+    nl[...] = STAT_DECAY * lstats[0] + (1.0 - STAT_DECAY) * term
+    put(9, nl, o_left.at[0])
+    mixed = dot(roots[0].astype(BF16), gb[...], 1, 0)
+    update = dot(mixed.astype(BF16), lroots[0].astype(BF16), 1, 1)
+    nk[...] = kt[0] - KERNEL_RATE * update
+    put(10, nk, o_kernel.at[0])
+    wholes = (stats.at[1], kt, nk, nl, bo, bg, momenta, params, nr, nl, nk)
+    for slot, whole in enumerate(wholes):
+        pltpu.make_async_copy(whole, whole, sem.at[slot]).wait()
 
 
 def room_of(size, kind, extra):
@@ -647,7 +696,6 @@
     dims = (nw, nn, pos, chan)
     hbm = pl.BlockSpec(memory_space=pl.ANY)
     vmem = pl.BlockSpec(memory_space=pltpu.VMEM)
-    span = -(-(share_width + 64) // 128) * 128
     board_shape = (SIDE, pos, SIDE, chan)
 
     kept = [
@@ -666,7 +714,7 @@
         sum(room_of(n * chan, kind, extra) for layer, n, kind in PIECES if layer == k)
         for k in range(2)
     )
-    transfers = sum(2 * len(kind) + 4 * kind.count("z") + extra for _, _, kind in PIECES)
+    flags = sum(len(kind) + 1 + 2 * extra for _, _, kind in PIECES)
     room = (49 + extra) * MIB // 2 + (ndev - 32) * 8 * chan * 4 + 8 * chan * max(arrivals - kin, 0)
     fused = pl.pallas_call(
         functools.partial(fused_kernel, dims),
@@ -681,7 +729,6 @@
             pltpu.VMEM((2, 2, chan), F32),
             pltpu.VMEM((chan, kin), F32),
             pltpu.VMEM((2, chan, kin), BF16),
-            pltpu.VMEM((span, chan), F32),
             pltpu.VMEM((rows + 2 * line, chunk), BF16),
             pltpu.VMEM((rows + 2 * line, chunk), BF16),
             pltpu.VMEM((rows + 2 * line, chunk), BF16),
@@ -693,11 +740,11 @@
             pltpu.VMEM((2, kin, chan), F32),
             pltpu.VMEM((4, ndev, 2, chan), F32),
             pltpu.VMEM((2, arrivals, chan), F32),
-            pltpu.SemaphoreType.DMA((25,)),
-            pltpu.SemaphoreType.DMA((4,)),
-            pltpu.SemaphoreType.DMA((4,)),
-            pltpu.SemaphoreType.DMA((transfers,)),
-            pltpu.SemaphoreType.DMA((transfers,)),
+            pltpu.SemaphoreType.DMA((13,)),
+            pltpu.SemaphoreType.DMA((1,)),
+            pltpu.SemaphoreType.DMA((2,)),
+            pltpu.SemaphoreType.DMA((len(PIECES),)),
+            pltpu.SemaphoreType.DMA((flags,)),
         ],
         compiler_params=pltpu.CompilerParams(
             collective_id=0, has_side_effects=True, vmem_limit_bytes=room
@@ -733,11 +780,11 @@
         in_specs=[vmem] * len(kept),
         out_specs=[hbm] * 8,
         scratch_shapes=[
-            pltpu.VMEM((2, kin, chan), BF16),
-            pltpu.VMEM((2, 3, share_width, chunk), F32),
-            pltpu.VMEM((2, share_width, chan), F32),
-            pltpu.VMEM((2, chan, chan), F32),
-            pltpu.SemaphoreType.DMA((32,)),
+            pltpu.VMEM((kin, chan), BF16),
+            pltpu.VMEM((3, share_width, chunk), F32),
+            pltpu.VMEM((share_width, chan), F32),
+            pltpu.VMEM((chan, chan), F32),
+            pltpu.SemaphoreType.DMA((11,)),
         ],
         compiler_params=pltpu.CompilerParams(vmem_limit_bytes=20 * MIB),
         name="finish",

time: 82.4 us -> 77.2 us (0.937)
  Pallas kernels: 81.3 us -> 76.2 us
    pallas_call x1, Pallas kernels: 74.2 us -> 70.8 us  [body(): fused(*(pltpu.with_memory_space_constraint(v, pltpu.HBM) for v in given))]
    pallas_call x1, Pallas kernels: 7.16 us -> 5.44 us  [body(): finish(*held)]
where the time goes in v3:
time: 77.2 us; the launch traced here: 77 us
  Pallas kernels  76.2 us (99%)
  between operations  0.81 us (1%)
    pallas_call x1, Pallas kernels, body(): fused(*(pltpu.with_memory_space_constraint(v, pltpu.HBM) for v in given))  70.8 us
    pallas_call x1, Pallas kernels, body(): finish(*held)  5.44 us

profile of v3, /device:TPU:0, one launch (start us, length us, event | category | flops | bytes accessed | tf_op | source)
XLA Modules:
  0.0 77.0 jit_solution(14685355846841997011)
XLA Ops:
  0.6 70.8 %fused_passes.1 = (f32[2,2304,256]{2,1,0:T(8,128)S(1)}, f32[2,576,2304]{2,1,0:T(8,128)S(1)}, f32[2,576,2304]{2,1,0:T(8,128)S(1)}, f32[2,256,256]{2,1,0:T(8,128)S...) custom-call(f32[12,8,8,256]{3,2,1,0:T(8,128)} %boards.1, ...), custom_call_target="tpu_custom_call" | custom-call | tf_op jit(solution)/shard_map/fused_passes/pallas_call | solution.py:766
  71.4 5.4 %finish.1 = (f32[12,8,8,256]{3,2,1,0:T(8,128)}, f32[12,8,8,256]{3,2,1,0:T(8,128)}, f32[2,576,256]{2,1,0:T(8,128)}, f32[2,576,256]{2,1,0:T(8,128)}, f32[2,256,256...) custom-call(f32[2,2304,256]{2,1,0:T(8,128)S(1)} %get-tuple-element.26.g_full, ...), custom_call_target="tpu_custom_call" | custom-call | tf_op jit(solution)/shard_map/finish/pallas_call | solution.py:792

commit v4 on v3

--- a/solution.py
+++ b/solution.py
@@ -24,21 +24,23 @@
 
 
 PIECES = (
-    (1, 1, "c12z"), (1, 1, "cz12"), (1, 1, "c12ab"), (1, 1, "cab12"),
-    (1, 1, "c12ab"), (1, 2, "c12z"), (1, 1, "c12ab"), (1, 1, "c12z"),
-    (0, 1, "c12ab"), (0, 1, "c12z"), (0, 1, "c12z"), (0, 1, "c12ab"),
-    (0, 1, "c12z"), (0, 2, "c12ab"), (0, 1, "c12z"), (0, 1, "cab12"),
+    (1, 1, "c12z"), (1, 1, "c12ab"), (1, 1, "c12z"), (1, 1, "cab12"),
+    (1, 1, "c12ab"), (1, 1, "c12ab"), (1, 1, "c12z"), (1, 1, "c12ab"),
+    (1, 1, "cz12"), (0, 1, "c12z"), (0, 1, "c12ab"), (0, 1, "c12z"),
+    (0, 1, "c12ab"), (0, 1, "cz12"), (0, 1, "c12z"), (0, 1, "c12z"),
+    (0, 1, "c12z"), (0, 1, "c12ab"),
 )
 ORDER = (
-    2, 6, 5, -1, 3, 2, -1, 6, -1, -2, 3, 5, 7, 1, 0, 4, 7, 4, 2, 1,
-    6, 3, 5, 0, -3, 8, 15, 13, 7, 2, 4, 6, 8, 15, 12, 10, 13, 5, 0, -4,
-    1, 12, 7, 11, 2, 9, 3, 4, 6, 8, 14, 11, 10, 15, 13, 0, 12, 9, 1, 4,
-    8, 2, 6, 3, 7, 11, 5, 14, 10, 13, 15, 12, 9, 4, 8, 11, 3, 2, 6, 0,
-    1, 14, 10, 15, 13, 7, 9, 5, -4, 1, 8, 4, 11, 12, 2, 15, 3, 6, 7, 14,
-    0, 13, 10, 5, -4, 4, 8, 9, 11, 15, 3, 2, 12, 0, -5, 13, 6, 14, 8, 15,
-    5, 4, 11, 10, 12, 7, 1, 9, 3, 13, 8, 14, 11, 0, 10, 2, 15, 4, 9, 12,
-    6, 13, 12, 7, 14, 6, 8, 11, 0, 3, 5, 1, 10, 9, 8, 3, 2, 4, 15, 1,
-    -7, -7, 13, 14, -7, 11, -7, 10, 15, 14, 9, 13, 11,
+    5, -1, -1, 4, -1, 5, -2, 7, 3, 4, 1, 6, 8, 0, 7, 3, 1, 6, 8, 0,
+    5, 2, 2, 4, 7, -3, 13, 3, 17, 1, 10, 16, 5, 6, 13, 17, 0, 10, 15, 12,
+    16, 7, 9, 2, 1, 5, 4, 6, 12, 8, 3, 0, 15, 17, 14, 7, 10, 9, 1, 2,
+    16, 5, 11, 4, 14, 13, 12, 8, 6, 17, 11, 3, 0, 15, 7, 1, 10, 16, 9, 5,
+    12, 2, 8, 14, 17, 4, 13, 3, 6, 15, 11, 10, 7, 1, 9, 5, 8, 12, 0, 14,
+    3, 13, 16, 6, 4, 17, 2, 11, 7, 1, 10, 15, 5, 13, 0, 9, 12, 4, 14, 3,
+    2, 16, 7, 17, -4, 11, 5, 1, 10, 6, 8, 15, 4, 9, 12, 16, 17, 14, 10, 3,
+    15, -4, 13, 0, 11, 7, 9, 1, 4, 12, 5, 6, 0, 17, 1, 2, 14, 7, 4, -4,
+    10, 8, 15, 11, 3, -5, 2, 12, 9, 3, 8, 16, 17, -7, -7, 10, 14, 13, -7, 11,
+    12, 17, -7, 10, 13, 14, 16, 9, 15, 11, 12,
 )
 
 

time: 77.2 us -> 75.8 us (0.982)
  Pallas kernels: 76.2 us -> 74.8 us
    pallas_call x1, Pallas kernels: 70.8 us -> 69.4 us  [body(): fused(*(pltpu.with_memory_space_constraint(v, pltpu.HBM) for v in given))]
where the time goes in v4:
time: 75.8 us; the launch traced here: 75.6 us
  Pallas kernels  74.8 us (99%)
  between operations  0.81 us (1%)
    pallas_call x1, Pallas kernels, body(): fused(*(pltpu.with_memory_space_constraint(v, pltpu.HBM) for v in given))  69.4 us
    pallas_call x1, Pallas kernels, body(): finish(*held)  5.44 us

profile of v4, /device:TPU:0, one launch (start us, length us, event | category | flops | bytes accessed | tf_op | source)
XLA Modules:
  0.0 75.6 jit_solution(1574172285670480555)
XLA Ops:
  0.6 69.4 %fused_passes.1 = (f32[2,2304,256]{2,1,0:T(8,128)S(1)}, f32[2,576,2304]{2,1,0:T(8,128)S(1)}, f32[2,576,2304]{2,1,0:T(8,128)S(1)}, f32[2,256,256]{2,1,0:T(8,128)S...) custom-call(f32[12,8,8,256]{3,2,1,0:T(8,128)} %boards.1, ...), custom_call_target="tpu_custom_call" | custom-call | tf_op jit(solution)/shard_map/fused_passes/pallas_call | solution.py:768
  70.0 5.4 %finish.1 = (f32[12,8,8,256]{3,2,1,0:T(8,128)}, f32[12,8,8,256]{3,2,1,0:T(8,128)}, f32[2,576,256]{2,1,0:T(8,128)}, f32[2,576,256]{2,1,0:T(8,128)}, f32[2,256,256...) custom-call(f32[2,2304,256]{2,1,0:T(8,128)S(1)} %get-tuple-element.26.g_full, ...), custom_call_target="tpu_custom_call" | custom-call | tf_op jit(solution)/shard_map/finish/pallas_call | solution.py:794

commit v5 on v4

--- a/solution.py
+++ b/solution.py
@@ -122,6 +122,7 @@
     rows = line * SIDE
     count = float(rows * nw * nn)
     chunk = 3 * chan
+    kin = 9 * chan
     wide, narrow = lax.axis_index("wide"), lax.axis_index("narrow")
     me = wide * nn + narrow
     extra_bits = list(range(3, nw.bit_length() - 1))
@@ -165,6 +166,8 @@
 
     def share(slot, value):
         red[slot, me] = value
+        if slot:
+            sent_all(slot - 1)
 
         def send(dev):
             pltpu.make_async_remote_copy(
@@ -181,8 +184,11 @@
     def collect(slot):
         others = red.at[slot, pl.ds(0, nw * nn - 1)]
         pltpu.make_async_copy(others, others, red_recv.at[slot % 2]).wait()
+        return red[slot]
+
+    def sent_all(slot):
+        others = red.at[slot, pl.ds(0, nw * nn - 1)]
         pltpu.make_async_copy(others, others, red_send.at[0]).wait()
-        return red[slot]
 
     def moments(slot):
         got = collect(slot)
@@ -303,8 +309,8 @@
         own = at(starts[-1], sizes[-1])
         flag = [g_recv.at[next(flags)] for _ in kind]
         back_flag = [g_recv.at[next(flags)]] + flag[:-1]
-        out_flag = g_send.at[len(sent)]
-        sent.append((k, 2 * (size - sizes[-1]), out_flag))
+        out_flag = g_send.at[k]
+        sent.append((k, 2 * (size - sizes[-1])))
 
         def scatter(i):
             part = sizes[i + 1]
@@ -598,8 +604,10 @@
         new_momenta[k] = value
         new_params[k] = par[k] - NORM_RATE * value
 
-    for k, size, out_flag in sent:
-        wait_for(gp.at[k, pl.ds(0, size)], out_flag)
+    sent_all(3)
+    for k in range(2):
+        size = sum(part for layer, part in sent if layer == k)
+        wait_for(stats_v.at[k, pl.ds(0, size * chan // kin)], g_send.at[k])
 
 
 def finish_kernel(
@@ -745,7 +753,7 @@
             pltpu.SemaphoreType.DMA((13,)),
             pltpu.SemaphoreType.DMA((1,)),
             pltpu.SemaphoreType.DMA((2,)),
-            pltpu.SemaphoreType.DMA((len(PIECES),)),
+            pltpu.SemaphoreType.DMA((2,)),
             pltpu.SemaphoreType.DMA((flags,)),
         ],
         compiler_params=pltpu.CompilerParams(

time: 75.8 us -> 75.6 us (level)
  no operation moved by 1% of the time
where the time goes in v5:
time: 75.6 us; the launch traced here: 75.5 us
  Pallas kernels  74.6 us (99%)
  between operations  0.81 us (1%)
    pallas_call x1, Pallas kernels, body(): fused(*(pltpu.with_memory_space_constraint(v, pltpu.HBM) for v in given))  69.2 us
    pallas_call x1, Pallas kernels, body(): finish(*held)  5.44 us

profile of v5, /device:TPU:0, one launch (start us, length us, event | category | flops | bytes accessed | tf_op | source)
XLA Modules:
  0.0 75.5 jit_solution(11100048622039320795)
XLA Ops:
  0.6 69.2 %fused_passes.1 = (f32[2,2304,256]{2,1,0:T(8,128)S(1)}, f32[2,576,2304]{2,1,0:T(8,128)S(1)}, f32[2,576,2304]{2,1,0:T(8,128)S(1)}, f32[2,256,256]{2,1,0:T(8,128)S...) custom-call(f32[12,8,8,256]{3,2,1,0:T(8,128)} %boards.1, ...), custom_call_target="tpu_custom_call" | custom-call | tf_op jit(solution)/shard_map/fused_passes/pallas_call | solution.py:776
  69.9 5.4 %finish.1 = (f32[12,8,8,256]{3,2,1,0:T(8,128)}, f32[12,8,8,256]{3,2,1,0:T(8,128)}, f32[2,576,256]{2,1,0:T(8,128)}, f32[2,576,256]{2,1,0:T(8,128)}, f32[2,256,256...) custom-call(f32[2,2304,256]{2,1,0:T(8,128)S(1)} %get-tuple-element.26.g_full, ...), custom_call_target="tpu_custom_call" | custom-call | tf_op jit(solution)/shard_map/finish/pallas_call | solution.py:802

commit v6 on v5

--- a/solution.py
+++ b/solution.py
@@ -24,23 +24,23 @@
 
 
 PIECES = (
-    (1, 1, "c12z"), (1, 1, "c12ab"), (1, 1, "c12z"), (1, 1, "cab12"),
-    (1, 1, "c12ab"), (1, 1, "c12ab"), (1, 1, "c12z"), (1, 1, "c12ab"),
-    (1, 1, "cz12"), (0, 1, "c12z"), (0, 1, "c12ab"), (0, 1, "c12z"),
-    (0, 1, "c12ab"), (0, 1, "cz12"), (0, 1, "c12z"), (0, 1, "c12z"),
+    (1, 1, "cab12"), (1, 1, "c12ab"), (1, 1, "c12z"), (1, 1, "cz12"),
+    (1, 1, "c12ab"), (1, 1, "c12ab"), (1, 1, "c12z"), (1, 1, "c12z"),
+    (1, 1, "c12z"), (0, 1, "c12ab"), (0, 1, "cz12"), (0, 1, "c12z"),
+    (0, 1, "c12z"), (0, 1, "c12z"), (0, 1, "c12ab"), (0, 1, "c12z"),
     (0, 1, "c12z"), (0, 1, "c12ab"),
 )
 ORDER = (
-    5, -1, -1, 4, -1, 5, -2, 7, 3, 4, 1, 6, 8, 0, 7, 3, 1, 6, 8, 0,
-    5, 2, 2, 4, 7, -3, 13, 3, 17, 1, 10, 16, 5, 6, 13, 17, 0, 10, 15, 12,
-    16, 7, 9, 2, 1, 5, 4, 6, 12, 8, 3, 0, 15, 17, 14, 7, 10, 9, 1, 2,
-    16, 5, 11, 4, 14, 13, 12, 8, 6, 17, 11, 3, 0, 15, 7, 1, 10, 16, 9, 5,
-    12, 2, 8, 14, 17, 4, 13, 3, 6, 15, 11, 10, 7, 1, 9, 5, 8, 12, 0, 14,
-    3, 13, 16, 6, 4, 17, 2, 11, 7, 1, 10, 15, 5, 13, 0, 9, 12, 4, 14, 3,
-    2, 16, 7, 17, -4, 11, 5, 1, 10, 6, 8, 15, 4, 9, 12, 16, 17, 14, 10, 3,
-    15, -4, 13, 0, 11, 7, 9, 1, 4, 12, 5, 6, 0, 17, 1, 2, 14, 7, 4, -4,
-    10, 8, 15, 11, 3, -5, 2, 12, 9, 3, 8, 16, 17, -7, -7, 10, 14, 13, -7, 11,
-    12, 17, -7, 10, 13, 14, 16, 9, 15, 11, 12,
+    5, -1, 0, 1, -1, 5, 4, -1, -2, 1, 0, 7, 3, 4, 2, 6, 7, 3, 2, 8,
+    6, 5, 8, 1, 0, -3, 10, 17, 12, 4, 7, 14, 15, 5, 2, 10, 17, 16, 9, 14,
+    6, 1, 12, 13, 4, 11, 8, 7, 9, 5, 0, 2, 15, 17, 6, -4, 13, 16, 1, 14,
+    4, 12, 8, 5, 9, 7, 3, 0, 17, 2, 15, 10, 11, 14, 6, -4, 4, 13, 1, 12,
+    9, 8, 0, 5, 16, 3, 7, 15, 14, 10, 17, 11, 2, 13, 4, 9, 6, 1, 16, 3,
+    0, 5, 12, 7, 8, 11, 10, 2, 14, 15, 17, 4, 1, 9, 3, 13, 5, 6, 16, 8,
+    12, 0, 14, 10, 11, 1, 17, 2, 15, 9, 4, 3, 13, 6, 12, 16, 5, 14, -4, 0,
+    17, 1, 15, 8, 11, 10, 13, 4, 9, 7, 16, 14, 4, 5, 2, 17, 3, 8, 11, 7,
+    0, 15, 6, 9, 12, 1, 13, 3, 16, 0, -7, 14, 12, -7, -7, 13, 17, 11, 10, 15,
+    16, 14, 9, -7, -5, 17, 11, 10, 9,
 )
 
 

time: 75.6 us -> 76 us (level)
  no operation moved by 1% of the time
where the time goes in v6:
time: 76 us; the launch traced here: 75.8 us
  Pallas kernels  75 us (99%)
  between operations  0.81 us (1%)
    pallas_call x1, Pallas kernels, body(): fused(*(pltpu.with_memory_space_constraint(v, pltpu.HBM) for v in given))  69.6 us
    pallas_call x1, Pallas kernels, body(): finish(*held)  5.44 us

profile of v6, /device:TPU:0, one launch (start us, length us, event | category | flops | bytes accessed | tf_op | source)
XLA Modules:
  0.0 75.8 jit_solution(8943598397333305837)
XLA Ops:
  0.6 69.6 %fused_passes.1 = (f32[2,2304,256]{2,1,0:T(8,128)S(1)}, f32[2,576,2304]{2,1,0:T(8,128)S(1)}, f32[2,576,2304]{2,1,0:T(8,128)S(1)}, f32[2,256,256]{2,1,0:T(8,128)S...) custom-call(f32[12,8,8,256]{3,2,1,0:T(8,128)} %boards.1, ...), custom_call_target="tpu_custom_call" | custom-call | tf_op jit(solution)/shard_map/fused_passes/pallas_call | solution.py:776
  70.2 5.4 %finish.1 = (f32[12,8,8,256]{3,2,1,0:T(8,128)}, f32[12,8,8,256]{3,2,1,0:T(8,128)}, f32[2,576,256]{2,1,0:T(8,128)}, f32[2,576,256]{2,1,0:T(8,128)}, f32[2,256,256...) custom-call(f32[2,2304,256]{2,1,0:T(8,128)S(1)} %get-tuple-element.26.g_full, ...), custom_call_target="tpu_custom_call" | custom-call | tf_op jit(solution)/shard_map/finish/pallas_call | solution.py:802
